TPU v7x, 32 devices: a whole 2x2x4 slice. The times are simulated.
32 devices in a mesh: dp: 8 (over z, x), tensor: 4 (over y, core).
Axes of the slice: x: 2, y: 2, z: 4, core: 2. Of those that a mesh axis runs over, the one named last changes fastest.
Arguments:
- layer_in: bfloat16 [8192, 768], P('dp'), may hold values from -6 to 6
- doc_ids: int32 [8192], P('dp'), may hold values from -1 to 8191, as said below
- qkv_weight: bfloat16 [3, 768, 768], P(None, None, 'tensor'), may hold values from -0.21875 to 0.21875
- out_weight: bfloat16 [768, 768], P('tensor'), may hold values from -1.25 to 1.25
- up_weight: bfloat16 [2, 768, 1152], P(None, None, 'tensor'), may hold values from -0.21875 to 0.21875
- down_weight: bfloat16 [1152, 768], P('tensor'), may hold values from -0.25 to 0.25
- norm1_gain: bfloat16 [768], replicated, may hold values from 0.5 to 1.5
- norm2_gain: bfloat16 [768], replicated, may hold values from 0.5 to 1.5
- out_cotangent: bfloat16 [8192, 768], P('dp'), may hold values from -6 to 6
Outputs:
- layer_out: bfloat16 [8192, 768], P('dp')
- input_grad: bfloat16 [8192, 768], P('dp')
- grad_qkv: float32 [3, 768, 768], P(None, None, 'tensor')
- grad_out: float32 [768, 768], P('tensor')
- grad_up: float32 [2, 768, 1152], P(None, None, 'tensor')
- grad_down: float32 [1152, 768], P('tensor')
- grad_norm1: float32 [768], replicated
- grad_norm2: float32 [768], replicated
Inputs may be any that keep to these rules, and one draw needn't show every extreme that they name: `doc_ids`: each aligned group of 1024 slots holds whole sequences of 1 to 512 tokens with increasing ids, followed by padding slots marked -1; ids are never shared by two groups; at least half of a group's slots are live, and some group has no padding.
All inputs are finite; a program needn't handle non-finite values.
Results may differ from a plain program's by a relative error of at most 0.013.
The roundings to bfloat16 on the way count: a program that leaves them out, or rounds other values in their place, can miss the bound.
Values sent between devices are 32-bit elements; how exact they have to be, the bound alone decides.
A program may use at most 128 MiB of HBM per device.

v0:
```python
import jax
import jax.numpy as jnp
from jax import lax
from jax.sharding import PartitionSpec as P

HD = 64
HALF = 64


def layer_norm(values, gain):
    row_mean = jnp.mean(values, axis=-1, keepdims=True)
    centred = values - row_mean
    variance = jnp.mean(centred * centred, axis=-1, keepdims=True)
    return centred * lax.rsqrt(variance + 1e-05) * gain


def exact_gelu(values):
    return jax.nn.gelu(values, approximate=False)


def tables(places):
    half_dim = HD // 2
    freqs = 10000.0 ** (-jnp.arange(half_dim, dtype=jnp.float32) * 2.0 / HD)
    angles = places.astype(jnp.float32)[:, None] * freqs[None, :]
    angles = jnp.concatenate([angles, angles], axis=-1)
    return (jnp.cos(angles), jnp.sin(angles))


def rotate(values, cosine_table, sine_table):
    half_dim = values.shape[-1] // 2
    turned = jnp.concatenate([-values[..., half_dim:], values[..., :half_dim]], axis=-1)
    return values * cosine_table[:, None, :] + turned * sine_table[:, None, :]


def window(array, block, fill):
    blocks = array.shape[0] // block
    widths = [(block, block)] + [(0, 0)] * (array.ndim - 1)
    padded = jnp.pad(array, widths, constant_values=fill)
    shaped = padded.reshape((blocks + 2, block) + array.shape[1:])
    return jnp.concatenate([shaped[:-2], shaped[1:-1], shaped[2:]], axis=1)


def fold_window(pieces, block):
    blocks = pieces.shape[0]
    rest = [(0, 0)] * (pieces.ndim - 1)
    middle_part = pieces[:, block : 2 * block]
    from_before = jnp.pad(pieces[:-1, 2 * block :], [(1, 0)] + rest)
    from_after = jnp.pad(pieces[1:, :block], [(0, 1)] + rest)
    whole = middle_part + from_before + from_after
    return whole.reshape((blocks * block,) + pieces.shape[2:])


def masked_scores(query_blocks, key_window, allowed):
    scores = jnp.einsum(
        "nqhd,nkhd->nhqk", query_blocks, key_window, preferred_element_type=jnp.float32
    ) * HD ** (-0.5)
    return jnp.where(allowed[:, None], scores, -1e30)


def per_device(
    layer_in,
    doc_ids,
    qkv_weight,
    out_weight,
    up_weight,
    down_weight,
    norm1_gain,
    norm2_gain,
    out_cotangent,
):
    token_rows = layer_in.shape[0]
    heads_local = qkv_weight.shape[2] // HD
    block = 2 * HALF
    blocks = token_rows // block
    slot_index = jnp.arange(token_rows, dtype=jnp.int32)
    previous = jnp.concatenate([doc_ids[:1] - 1, doc_ids[:-1]])
    starts = jnp.where(doc_ids != previous, slot_index, 0)
    places = slot_index - lax.cummax(starts, axis=0)
    cosine_table, sine_table = tables(places)
    query_slots = slot_index.reshape(blocks, block)
    key_slots = (
        jnp.arange(blocks, dtype=jnp.int32)[:, None] * block
        - block
        + jnp.arange(3 * block, dtype=jnp.int32)[None, :]
    )
    query_docs = doc_ids.reshape(blocks, block)
    key_docs = window(doc_ids, block, -2)
    distance = jnp.abs(query_slots[:, :, None] - key_slots[:, None, :])
    same_doc = (query_docs[:, :, None] == key_docs[:, None, :]) & (query_docs[:, :, None] >= 0)
    allowed = same_doc & (distance <= HALF) | (distance == 0)

    def turn(values):
        return rotate(values.reshape(token_rows, heads_local, HD), cosine_table, sine_table)

    layer_float = layer_in.astype(jnp.float32)
    normed_one, norm_one_pull = jax.vjp(layer_norm, layer_float, norm1_gain.astype(jnp.float32))
    hidden_one = normed_one.astype(jnp.bfloat16)
    projected = jnp.einsum(
        "td,cde->cte", hidden_one, qkv_weight, preferred_element_type=jnp.float32
    )
    query_float, query_pull = jax.vjp(turn, projected[0])
    key_float, key_pull = jax.vjp(turn, projected[1])
    query = query_float.astype(jnp.bfloat16)
    keys_rot = key_float.astype(jnp.bfloat16)
    values = projected[2].reshape(token_rows, heads_local, HD).astype(jnp.bfloat16)
    query_blocks = query.reshape(blocks, block, heads_local, HD)
    key_window = window(keys_rot, block, 0)
    value_window = window(values, block, 0)
    scores = masked_scores(query_blocks, key_window, allowed)
    top_score = jnp.max(scores, axis=-1, keepdims=True)
    expo = jnp.exp(scores - top_score)
    total = jnp.sum(expo, axis=-1, keepdims=True)
    probs = expo / total
    log_total = top_score + jnp.log(total)
    attended = jnp.einsum(
        "nhqk,nkhd->nqhd",
        probs.astype(jnp.bfloat16),
        value_window,
        preferred_element_type=jnp.float32,
    )
    attended = attended.reshape(token_rows, -1).astype(jnp.bfloat16)
    attn_part = jnp.dot(attended, out_weight, preferred_element_type=jnp.float32)
    attn_branch = lax.psum(attn_part, "tensor")
    middle = layer_float + attn_branch
    normed_two, norm_two_pull = jax.vjp(layer_norm, middle, norm2_gain.astype(jnp.float32))
    hidden_two = normed_two.astype(jnp.bfloat16)
    up_parts = jnp.einsum("td,cdf->ctf", hidden_two, up_weight, preferred_element_type=jnp.float32)
    gate_in = up_parts[0]
    gate_up = up_parts[1]
    gelu_value, gelu_pull = jax.vjp(exact_gelu, gate_in)
    activated = (gelu_value * gate_up).astype(jnp.bfloat16)
    mlp_part = jnp.dot(activated, down_weight, preferred_element_type=jnp.float32)
    mlp_branch = lax.psum(mlp_part, "tensor")
    layer_out = (middle + mlp_branch).astype(jnp.bfloat16)
    cot_float = out_cotangent.astype(jnp.float32)
    grad_down = jnp.einsum(
        "tf,td->fd", activated, out_cotangent, preferred_element_type=jnp.float32
    )
    grad_act = jnp.einsum(
        "td,fd->tf", out_cotangent, down_weight, preferred_element_type=jnp.float32
    )
    grad_gate_in = gelu_pull(grad_act * gate_up)[0]
    grad_gate_up = grad_act * gelu_value
    grad_up_parts = jnp.stack([grad_gate_in, grad_gate_up]).astype(jnp.bfloat16)
    grad_up = jnp.einsum(
        "td,ctf->cdf", hidden_two, grad_up_parts, preferred_element_type=jnp.float32
    )
    hidden_two_part = jnp.einsum(
        "ctf,cdf->td", grad_up_parts, up_weight, preferred_element_type=jnp.float32
    )
    grad_hidden_two = lax.psum(hidden_two_part, "tensor")
    grad_middle_norm, grad_gain_two = norm_two_pull(grad_hidden_two)
    grad_middle = cot_float + grad_middle_norm
    grad_branch = grad_middle.astype(jnp.bfloat16)
    grad_out = jnp.einsum("te,td->ed", attended, grad_branch, preferred_element_type=jnp.float32)
    grad_attended = jnp.einsum(
        "td,ed->te", grad_branch, out_weight, preferred_element_type=jnp.float32
    )
    grad_attended = grad_attended.reshape(blocks, block, heads_local, HD).astype(jnp.bfloat16)
    probs_again = jnp.exp(masked_scores(query_blocks, key_window, allowed) - log_total)
    grad_value_window = jnp.einsum(
        "nhqk,nqhd->nkhd",
        probs_again.astype(jnp.bfloat16),
        grad_attended,
        preferred_element_type=jnp.float32,
    )
    grad_probs = jnp.einsum(
        "nqhd,nkhd->nhqk", grad_attended, value_window, preferred_element_type=jnp.float32
    )
    grad_scores = probs_again * (
        grad_probs - jnp.sum(probs_again * grad_probs, axis=-1, keepdims=True)
    )
    grad_scores = grad_scores.astype(jnp.bfloat16)
    grad_query = jnp.einsum(
        "nhqk,nkhd->nqhd", grad_scores, key_window, preferred_element_type=jnp.float32
    ) * HD ** (-0.5)
    grad_key_window = jnp.einsum(
        "nhqk,nqhd->nkhd", grad_scores, query_blocks, preferred_element_type=jnp.float32
    ) * HD ** (-0.5)
    grad_query = grad_query.reshape(token_rows, heads_local, HD)
    grad_keys = fold_window(grad_key_window, block)
    grad_values = fold_window(grad_value_window, block)
    grad_query_proj = query_pull(grad_query)[0]
    grad_key_proj = key_pull(grad_keys)[0]
    grad_value_proj = grad_values.reshape(token_rows, -1)
    grad_projected = jnp.stack([grad_query_proj, grad_key_proj, grad_value_proj]).astype(
        jnp.bfloat16
    )
    grad_qkv = jnp.einsum(
        "td,cte->cde", hidden_one, grad_projected, preferred_element_type=jnp.float32
    )
    hidden_one_part = jnp.einsum(
        "cte,cde->td", grad_projected, qkv_weight, preferred_element_type=jnp.float32
    )
    grad_hidden_one = lax.psum(hidden_one_part, "tensor")
    grad_input_norm, grad_gain_one = norm_one_pull(grad_hidden_one)
    input_grad = (grad_middle + grad_input_norm).astype(jnp.bfloat16)
    grad_qkv, grad_out, grad_up, grad_down, grad_gain_one, grad_gain_two = lax.psum(
        (grad_qkv, grad_out, grad_up, grad_down, grad_gain_one, grad_gain_two), "dp"
    )
    return (
        layer_out,
        input_grad,
        grad_qkv,
        grad_out,
        grad_up,
        grad_down,
        grad_gain_one,
        grad_gain_two,
    )


def solution(mesh):
    return jax.shard_map(
        per_device,
        mesh=mesh,
        in_specs=(
            P("dp", None),
            P("dp"),
            P(None, None, "tensor"),
            P("tensor", None),
            P(None, None, "tensor"),
            P("tensor", None),
            P(),
            P(),
            P("dp", None),
        ),
        out_specs=(
            P("dp", None),
            P("dp", None),
            P(None, None, "tensor"),
            P("tensor", None),
            P(None, None, "tensor"),
            P("tensor", None),
            P(),
            P(),
        ),
        check_vma=False,
    )
```

profile of v0, /device:TPU:0, one launch (start us, length us, event | category | flops | bytes accessed | tf_op | source)
XLA Modules:
  0.0 530.8 jit_solution(14084247363405428457)
XLA Ops:
  7.2 1.4 slice.128
  9.3 0.9 select_bitcast_fusion
  10.9 0.7 broadcast_compare_fusion
  11.5 1.7 convert_reduce_fusion
  13.2 0.6 fusion.10
  13.9 0.6 copy-done.51
  14.5 1.3 fusion.108
  16.7 1.0 fusion.90
  18.6 1.9 fusion.88
  22.2 1.0 fusion.26
  23.6 1.1 fusion.118
  24.8 1.2 fusion.4
  26.4 0.6 copy-done.4
  26.9 1.7 fusion.32
  28.9 2.3 fusion.78
  32.3 3.1 fusion.120
  35.4 67.2 %all-reduce.19.cloned.1.call-done = f32[1024,768]{1,0:T(8,128)} async-done(((f32[1024,768]{1,0:T(8,128)}), f32[1024,768]{1,0:T(8,128)}) %all-reduce.19.cloned.1.call-update) | async-done | bytes 3145744 | tf_op jit(solution)/shard_map/psum | solution.py:123
  102.6 2.3 fusion.113
  104.9 0.5 multiply_reduce_fusion.3
  105.4 1.3 copy-done.62
  106.7 1.3 convolution_bitcast_fusion.2
  108.0 2.8 fusion.71
  110.8 0.6 fusion.70
  111.6 0.6 copy-done.33
  112.2 3.1 convolution_bitcast_fusion.1
  115.6 3.8 fusion.119
  119.4 64.6 %all-reduce.21.cloned.1.call-done = f32[1024,768]{1,0:T(8,128)} async-done(((f32[1024,768]{1,0:T(8,128)}), f32[1024,768]{1,0:T(8,128)}) %all-reduce.21.cloned.1.call-update) | async-done | bytes 3145744 | tf_op jit(solution)/shard_map/psum | solution.py:151
  184.0 4.5 multiply_reduce_fusion.1
  188.7 1.4 fusion.111
  190.1 0.4 fusion.16
  190.6 1.2 copy-done.6
  191.8 0.7 fusion.33
  192.5 1.5 slice-done
  194.5 1.8 multiply_reduce_fusion
  196.3 1.1 multiply_convert_fusion
  197.5 0.6 multiply_bitcast_fusion
  198.7 1.2 fusion.30
  199.9 1.2 fusion.17
  201.3 0.8 copy-done.23
  202.4 0.9 fusion.116
  203.3 1.0 fusion.117
  204.6 1.0 copy.39
  205.6 1.9 stack_reshape_reshape.4
  207.5 2.5 fusion.59
  210.1 0.7 copy-done.46
  210.9 3.1 convolution_bitcast_fusion
  214.3 0.7 copy-done.20
  215.0 3.1 fusion.121
  218.2 2.6 convolution_bitcast_fusion.3
  220.8 1.3 fusion.76
  222.1 2.5 fusion.27
  224.6 109.5 %all-reduce.25.cloned.1.call-done = (f32[1024,768]{1,0:T(8,128)}, f32[1024,768]{1,0:T(8,128)}) async-done(((f32[1024,768]{1,0:T(8,128)}, f32[1024,768]{1,0:T(8,128)}), (f32[1024,768]{1,0:T(8,128)}, f32[1024,768]{1,0:T(8,128)})) %all-reduce.25.cloned.1.call-update) | async-done | bytes 6291472 | tf_op jit(solution)/shard_map/psum | solution.py:133
  334.1 2.8 fusion.11
  336.9 1.7 fusion.9
  338.6 23.1 %all-reduce.11 = (f32[768]{0:T(1024)}, f32[768]{0:T(1024)}) all-reduce(f32[768]{0:T(1024)S(1)} %get-tuple-element.10, f32[768]{0:T(1024)S(1)} %copy-done.59), channel_id=1, replica_groups=mesh['dp'=8,'tensor'=4] {'dp'}, use_global_device_ids=true, to_apply=%region_22.23 | all-reduce | flops 1536 | bytes 12288 | tf_op jit(solution)/shard_map/psum | solution.py:198
  361.7 4.5 add_convert_fusion.1
  366.2 0.8 copy-done.9
  367.5 2.3 add_convert_fusion
  369.8 147.9 %all-reduce.23.cloned.1.call-done = (f32[3,768,192]{1,2,0:T(8,128)}, f32[192,768]{1,0:T(8,128)}, f32[2,768,288]{1,2,0:T(8,128)}, f32[288,768]{1,0:T(8,128)}) async-done(((f32[3,768,192]{1,2,0:T(8,128)}, f32[192,768]{1,0:T(8,128)}, f32[2,768,288]{1,2,0:T(8,128)}, f32[288,768]{1,0:T(8,128)}), (f32[3,768,192]{1,2,0:T(8,128)}, f32[192,768]{1,0:T(8,128)}, f32[2,768,288]{1,2,0:T(8,128)}, ...) | async-done | bytes 5013520 | tf_op jit(solution)/shard_map/psum | solution.py:198
  517.8 2.9 copy.99
  520.7 0.8 copy.100
  521.5 1.2 copy.101
  522.7 0.6 copy-done.32
  523.3 0.9 copy.102
  (179 shorter events, 9.8 us)
Async XLA Ops:
  7.2 7.3 %copy-start = (bf16[3,768,192]{1,2,0:T(8,128)(2,1)S(1)}, bf16[3,768,192]{1,2,0:T(8,128)(2,1)}, u32[]{:S(2)}) copy-start(bf16[3,768,192]{1,2,0:T(8,128)(2,1)} %param.11) | copy-start | bytes 2654212
  7.2 6.1 %copy-start.5 = (bf16[1024,768]{1,0:T(8,128)(2,1)S(1)}, bf16[1024,768]{1,0:T(8,128)(2,1)}, u32[]{:S(2)}) copy-start(bf16[1024,768]{1,0:T(8,128)(2,1)} %param.9) | copy-start | bytes 4718596
  7.2 7.3 %copy-start.60 = (bf16[768]{0:T(1024)(128)(2,1)S(1)}, bf16[768]{0:T(1024)(128)(2,1)}, u32[]{:S(2)}) copy-start(bf16[768]{0:T(1024)(128)(2,1)} %param.15) | copy-start | bytes 4612
  7.2 95.4 %all-reduce.19.cloned.1.call-start = ((), (), s32[]{:S(2)}) async-start(), calls=%async_computation | async-start | bytes 6291456 | tf_op jit(solution)/shard_map/psum | solution.py:123
  17.7 0.8 copy-start.22
  21.8 1.8 copy-start.42
  21.8 1.8 copy-start.44
  23.5 1.3 copy-start.38
  23.6 1.2 copy-start.28
  24.8 2.2 copy-start.4
  26.9 1.7 copy-start.24
  26.9 2.0 copy-start.30
  31.3 1.0 copy-start.27
  31.3 152.7 %all-reduce.21.cloned.1.call-start = ((), (), s32[]{:S(2)}) async-start(), calls=%async_computation.1 | async-start | bytes 6291456 | tf_op jit(solution)/shard_map/psum | solution.py:151
  32.3 156.2 %copy-start.55 = (f32[768]{0:T(1024)}, f32[768]{0:T(1024)S(1)}, u32[]{:S(2)}) copy-start(f32[768]{0:T(1024)S(1)} %convert_element_type.110) | copy-start | bytes 9220
  104.9 3.1 copy-start.1
  104.9 1.8 copy-start.62
  106.7 81.9 %copy-start.57 = (f32[1024]{0:T(1024)}, f32[1024]{0:T(1024)S(1)}, u32[]{:S(2)}) copy-start(f32[1024]{0:T(1024)S(1)} %fusion.97) | copy-start | bytes 12292
  106.7 1.3 copy-start.16
  110.8 0.8 copy-start.36
  111.4 0.8 copy-start.33
  111.4 4.2 copy-start.19
  115.3 218.7 %all-reduce.25.cloned.1.call-start = ((), (), s32[]{:S(2)}) async-start(), calls=%async_computation.3 | async-start | bytes 12582912 | tf_op jit(solution)/shard_map/psum | solution.py:133
  184.0 4.6 copy-start.2
  184.0 4.7 copy-start.14
  188.7 1.4 copy-start.10
  190.1 1.7 copy-start.6
  190.1 1.7 copy-start.53
  190.1 4.0 slice-start
  190.1 1.7 copy-start.31
  190.1 4.0 slice-start.1
  191.8 4.5 copy-start.12
  191.8 2.7 copy-start.25
  196.3 1.1 copy-start.29
  197.4 1.0 copy-start.39
  197.4 1.1 copy-start.43
  197.5 1.2 copy-start.45
  198.7 2.6 copy-start.15
  199.9 1.4 copy-start.18
  201.1 1.0 copy-start.23
  201.3 1.1 copy-start.17
  207.5 3.4 copy-start.40
  210.0 0.9 copy-start.48
  214.0 1.1 copy-start.20
  214.0 4.1 copy-start.56
  214.0 4.1 copy-start.58
  214.0 303.7 %all-reduce.23.cloned.1.call-start = ((), (), s32[]{:S(2)}) async-start(), calls=%async_computation.2 | async-start | bytes 10027008 | tf_op jit(solution)/shard_map/psum | solution.py:198
  215.0 3.1 copy-start.3
  215.0 3.1 copy-start.34
  215.0 3.1 copy-start.37
  218.2 2.6 copy-start.13
  220.7 1.3 copy-start.41
  220.7 1.3 copy-start.47
  220.7 1.3 copy-start.49
  334.1 2.8 copy-start.52
  334.1 2.8 copy-start.8
  336.9 1.7 copy-start.59
  336.9 29.3 %copy-start.54 = (f32[1024]{0:T(1024)S(1)}, f32[1024]{0:T(1024)}, u32[]{:S(2)}) copy-start(f32[1024]{0:T(1024)} %copy-done.53) | copy-start | bytes 12292
  361.7 4.5 copy-start.7
  361.7 5.3 %copy-start.9 = (f32[1024,768]{1,0:T(8,128)S(1)}, f32[1024,768]{1,0:T(8,128)}, u32[]{:S(2)}) copy-start(f32[1024,768]{1,0:T(8,128)} %get-tuple-element.19) | copy-start | bytes 9437188
  361.7 5.8 %copy-start.11 = (bf16[1024,768]{1,0:T(8,128)(2,1)S(1)}, bf16[1024,768]{1,0:T(8,128)(2,1)}, u32[]{:S(2)}) copy-start(bf16[1024,768]{1,0:T(8,128)(2,1)} %param.17) | copy-start | bytes 4718596
  517.8 3.0 copy-start.35
  517.8 3.8 copy-start.26
  521.5 1.8 copy-start.32
  (5 other events, 3.4 us)
Sparse Core Ops, SparseCore 0:
  31.4 71.1 all-reduce.18
  115.4 68.5 all-reduce.20
  214.1 119.8 all-reduce.24
  338.5 179.2 all-reduce.22
where the time goes:
time: 531 us
  waiting for transfers between devices  389 us (73%)
  other arithmetic  40.1 us (8%)
  matrix products  35.6 us (7%)
  local copies, waits for them, and re-layouts  26.5 us (5%)
  blocking collectives  23.1 us (4%)
  between operations  15.3 us (3%)
    psum x1, waiting for transfers between devices, per_device(): lax.psum((grad_qkv, grad_out, grad_up, grad_down, grad_gain_one, grad_gai...  148 us
    psum x1, waiting for transfers between devices, per_device(): mlp_branch = lax.psum(mlp_part, 'tensor')  109 us
    psum x1, waiting for transfers between devices, per_device(): attn_branch = lax.psum(attn_part, 'tensor')  67.2 us
    psum x1, waiting for transfers between devices, per_device(): grad_hidden_two = lax.psum(hidden_two_part, 'tensor')  64.6 us
    psum x1, blocking collectives, per_device(): lax.psum((grad_qkv, grad_out, grad_up, grad_down, grad_gain_one, grad_gai...  23.1 us
    unnamed x146, local copies, waits for them, and re-layouts  20.6 us
  transfers between devices with their start and end apart: 4, of which 4 were waited for; matrix products, arithmetic and copies ran while one was open for 5% of the time, Pallas kernels for 0%

commit v1 on v0

v1 whole, which is shorter than its diff:
```python
import functools

import jax
import jax.numpy as jnp
from jax import lax
from jax.sharding import PartitionSpec as P

HD = 64
HALF = 64


def layer_norm(values, gain):
    row_mean = jnp.mean(values, axis=-1, keepdims=True)
    centred = values - row_mean
    variance = jnp.mean(centred * centred, axis=-1, keepdims=True)
    return centred * lax.rsqrt(variance + 1e-05) * gain


def exact_gelu(values):
    return jax.nn.gelu(values, approximate=False)


def tables(places):
    half_dim = HD // 2
    freqs = 10000.0 ** (-jnp.arange(half_dim, dtype=jnp.float32) * 2.0 / HD)
    angles = places.astype(jnp.float32)[:, None] * freqs[None, :]
    angles = jnp.concatenate([angles, angles], axis=-1)
    return (jnp.cos(angles), jnp.sin(angles))


def rotate(values, cosine_table, sine_table):
    half_dim = values.shape[-1] // 2
    turned = jnp.concatenate([-values[..., half_dim:], values[..., :half_dim]], axis=-1)
    return values * cosine_table[:, None, :] + turned * sine_table[:, None, :]


def window(array, block, fill):
    blocks = array.shape[0] // block
    widths = [(block, block)] + [(0, 0)] * (array.ndim - 1)
    padded = jnp.pad(array, widths, constant_values=fill)
    shaped = padded.reshape((blocks + 2, block) + array.shape[1:])
    return jnp.concatenate([shaped[:-2], shaped[1:-1], shaped[2:]], axis=1)


def fold_window(pieces, block):
    blocks = pieces.shape[0]
    rest = [(0, 0)] * (pieces.ndim - 1)
    middle_part = pieces[:, block : 2 * block]
    from_before = jnp.pad(pieces[:-1, 2 * block :], [(1, 0)] + rest)
    from_after = jnp.pad(pieces[1:, :block], [(0, 1)] + rest)
    whole = middle_part + from_before + from_after
    return whole.reshape((blocks * block,) + pieces.shape[2:])


def masked_scores(query_blocks, key_window, allowed):
    scores = jnp.einsum(
        "nqhd,nkhd->nhqk", query_blocks, key_window, preferred_element_type=jnp.float32
    ) * HD ** (-0.5)
    return jnp.where(allowed[:, None], scores, -1e30)


def swap(array, axis, mask, size):
    return lax.ppermute(array, axis, [(i, i ^ mask) for i in range(size)])


def halve(array):
    return array * 0.5


def rows_of(array, part, rows):
    return lax.dynamic_slice_in_dim(array, part * rows, rows, axis=0)


def place_two(mine, other, bit):
    both = jnp.zeros((2,) + mine.shape, mine.dtype)
    both = lax.dynamic_update_index_in_dim(both, mine, bit, 0)
    return lax.dynamic_update_index_in_dim(both, other, 1 - bit, 0)


def halving_sum(buffer, me, masks, size):
    for mask in masks:
        bit = (me // mask) % 2
        half = buffer.shape[0] // 2
        sent = rows_of(buffer, 1 - bit, half)
        kept = rows_of(buffer, bit, half)
        buffer = kept + swap(sent, "dp", mask, size)
    for mask in reversed(masks):
        bit = (me // mask) % 2
        other = swap(buffer, "dp", mask, size)
        buffer = place_two(buffer, other, bit).reshape((-1,) + buffer.shape[1:])
    return buffer


def dp_sum(pieces, me, size):
    rows = sum(piece.shape[0] for piece in pieces)
    unit = 16 * size
    padded = -(-rows // unit) * unit
    if padded > rows:
        pieces = list(pieces) + [jnp.zeros((padded - rows, pieces[0].shape[1]), jnp.float32)]
    whole = jnp.concatenate(pieces, axis=0)
    masks = []
    mask = 1
    while mask < size:
        masks.append(mask)
        mask *= 2
    cut = padded // 2
    first = halving_sum(whole[:cut], me, masks, size)
    second = halving_sum(whole[cut:], me, masks[1:] + masks[:1], size)
    return jnp.concatenate([first, second], axis=0)[:rows]


def per_device(
    tensor_size,
    dp_size,
    layer_in,
    doc_ids,
    qkv_weight,
    out_weight,
    up_weight,
    down_weight,
    norm1_gain,
    norm2_gain,
    out_cotangent,
):
    token_rows, width = layer_in.shape
    heads_local = qkv_weight.shape[2] // HD
    columns = heads_local * HD
    block = 2 * HALF
    blocks = token_rows // block
    half_rows = token_rows // 2
    lane = lax.axis_index("tensor")
    me = lax.axis_index("dp")
    core = lane % 2
    bfloat = jnp.bfloat16
    float32 = jnp.float32

    def across(array, mask):
        return swap(array, "tensor", mask, tensor_size)

    weight_float = out_weight.astype(float32) * 2.0
    weight_two = across(weight_float, 2)
    weight_one = across(weight_float, 1)
    weight_three = across(weight_two, 1)
    out_full = jnp.zeros((tensor_size,) + out_weight.shape, bfloat)
    out_full = lax.dynamic_update_index_in_dim(out_full, out_weight, lane, 0)
    for mask, piece in ((1, weight_one), (2, weight_two), (3, weight_three)):
        out_full = lax.dynamic_update_index_in_dim(
            out_full, halve(piece).astype(bfloat), lane ^ mask, 0
        )

    slot_index = jnp.arange(token_rows, dtype=jnp.int32)
    previous = jnp.concatenate([doc_ids[:1] - 1, doc_ids[:-1]])
    starts = jnp.where(doc_ids != previous, slot_index, 0)
    places = slot_index - lax.cummax(starts, axis=0)
    cosine_table, sine_table = tables(places)
    query_slots = slot_index.reshape(blocks, block)
    key_slots = (
        jnp.arange(blocks, dtype=jnp.int32)[:, None] * block
        - block
        + jnp.arange(3 * block, dtype=jnp.int32)[None, :]
    )
    query_docs = doc_ids.reshape(blocks, block)
    key_docs = window(doc_ids, block, -2)
    distance = jnp.abs(query_slots[:, :, None] - key_slots[:, None, :])
    same_doc = (query_docs[:, :, None] == key_docs[:, None, :]) & (query_docs[:, :, None] >= 0)
    allowed = same_doc & (distance <= HALF) | (distance == 0)

    def turn(values):
        return rotate(values.reshape(token_rows, heads_local, HD), cosine_table, sine_table)

    gain_one = norm1_gain.astype(float32)
    gain_two = norm2_gain.astype(float32)
    layer_float = layer_in.astype(float32)
    hidden_one = layer_norm(layer_float, gain_one).astype(bfloat)
    projected = jnp.einsum("td,cde->cte", hidden_one, qkv_weight, preferred_element_type=float32)
    query_float, query_pull = jax.vjp(turn, projected[0])
    key_float, key_pull = jax.vjp(turn, projected[1])
    query = query_float.astype(bfloat)
    keys_rot = key_float.astype(bfloat)
    values = projected[2].reshape(token_rows, heads_local, HD).astype(bfloat)
    query_blocks = query.reshape(blocks, block, heads_local, HD)
    key_window = window(keys_rot, block, 0)
    value_window = window(values, block, 0)
    scores = masked_scores(query_blocks, key_window, allowed)
    top_score = jnp.max(scores, axis=-1, keepdims=True)
    expo = jnp.exp(scores - top_score)
    total = jnp.sum(expo, axis=-1, keepdims=True)
    probs = expo / total
    log_total = top_score + jnp.log(total)
    attended = jnp.einsum(
        "nhqk,nkhd->nqhd", probs.astype(bfloat), value_window, preferred_element_type=float32
    )
    attended_float = attended.reshape(token_rows, columns)
    attended = attended_float.astype(bfloat)

    attended_mine = rows_of(attended, core, half_rows)
    doubled = attended_float * 2.0
    float_mine = rows_of(doubled, core, half_rows)
    float_other = rows_of(doubled, 1 - core, half_rows)
    from_three = across(float_other, 3)
    from_two = across(float_mine, 2)
    from_one = across(float_other, 1)
    all_heads = jnp.zeros((tensor_size, half_rows, columns), bfloat)
    all_heads = lax.dynamic_update_index_in_dim(all_heads, attended_mine, lane, 0)
    for mask, piece in ((1, from_one), (2, from_two), (3, from_three)):
        all_heads = lax.dynamic_update_index_in_dim(
            all_heads, halve(piece).astype(bfloat), lane ^ mask, 0
        )
    attn_branch = jnp.einsum("jte,jed->td", all_heads, out_full, preferred_element_type=float32)
    layer_mine = rows_of(layer_float, core, half_rows)
    layer_other = rows_of(layer_float, 1 - core, half_rows)
    middle = layer_mine + attn_branch
    norm_two_pull = jax.vjp(lambda rows: layer_norm(rows, gain_two), middle)[1]
    normed_two = layer_norm(middle, 1.0)
    hidden_mine = (normed_two * gain_two).astype(bfloat)
    hidden_other = (across(normed_two, 1) * gain_two).astype(bfloat)
    hidden_two = place_two(hidden_mine, hidden_other, core).reshape(token_rows, width)

    up_parts = jnp.einsum("td,cdf->ctf", hidden_two, up_weight, preferred_element_type=float32)
    gate_in = up_parts[0]
    gate_up = up_parts[1]
    gelu_value, gelu_pull = jax.vjp(exact_gelu, gate_in)
    activated = (gelu_value * gate_up).astype(bfloat)
    grad_act = jnp.einsum("td,fd->tf", out_cotangent, down_weight, preferred_element_type=float32)
    grad_gate_in = gelu_pull(grad_act * gate_up)[0]
    grad_gate_up = grad_act * gelu_value
    grad_up_parts = jnp.stack([grad_gate_in, grad_gate_up], axis=1).astype(bfloat)

    def tensor_sum(product, rows_in):
        part_other = product(rows_of(rows_in, 1 - core, half_rows))
        arrived = across(part_other, 1)
        part_mine = product(rows_of(rows_in, core, half_rows))
        mine = part_mine + arrived
        return mine + across(mine, 2)

    grad_hidden_two = tensor_sum(
        lambda rows: jnp.einsum("tcf,cdf->td", rows, up_weight, preferred_element_type=float32),
        grad_up_parts,
    )
    cot_mine = rows_of(out_cotangent, core, half_rows).astype(float32)
    cot_other = rows_of(out_cotangent, 1 - core, half_rows).astype(float32)
    norm_two_part = norm_two_pull(grad_hidden_two)[0]
    branch_mine = (cot_mine + norm_two_part).astype(bfloat)
    branch_other = (cot_other + across(norm_two_part, 1)).astype(bfloat)
    grad_branch = place_two(branch_mine, branch_other, core).reshape(token_rows, width)

    mlp_branch = tensor_sum(
        lambda rows: jnp.dot(rows, down_weight, preferred_element_type=float32), activated
    )
    both_branches = attn_branch + mlp_branch
    out_mine = (layer_mine + both_branches).astype(bfloat)
    out_other = (layer_other + across(both_branches, 1)).astype(bfloat)
    layer_out = place_two(out_mine, out_other, core).reshape(token_rows, width)

    grad_down = jnp.einsum("tf,td->fd", activated, out_cotangent, preferred_element_type=float32)
    grad_up = jnp.einsum("td,tcf->cfd", hidden_two, grad_up_parts, preferred_element_type=float32)
    units = grad_down.shape[0]
    gain_grad_two = jnp.einsum("cfd,cdf->d", grad_up, up_weight.astype(float32)) / gain_two

    grad_out = jnp.einsum("te,td->ed", attended, grad_branch, preferred_element_type=float32)
    grad_attended = jnp.einsum("td,ed->te", grad_branch, out_weight, preferred_element_type=float32)
    grad_attended = grad_attended.reshape(blocks, block, heads_local, HD).astype(bfloat)
    probs_again = jnp.exp(masked_scores(query_blocks, key_window, allowed) - log_total)
    grad_value_window = jnp.einsum(
        "nhqk,nqhd->nkhd", probs_again.astype(bfloat), grad_attended, preferred_element_type=float32
    )
    grad_probs = jnp.einsum(
        "nqhd,nkhd->nhqk", grad_attended, value_window, preferred_element_type=float32
    )
    grad_scores = probs_again * (
        grad_probs - jnp.sum(probs_again * grad_probs, axis=-1, keepdims=True)
    )
    grad_scores = grad_scores.astype(bfloat)
    grad_query = jnp.einsum(
        "nhqk,nkhd->nqhd", grad_scores, key_window, preferred_element_type=float32
    ) * HD ** (-0.5)
    grad_key_window = jnp.einsum(
        "nhqk,nqhd->nkhd", grad_scores, query_blocks, preferred_element_type=float32
    ) * HD ** (-0.5)
    grad_query = grad_query.reshape(token_rows, heads_local, HD)
    grad_keys = fold_window(grad_key_window, block)
    grad_values = fold_window(grad_value_window, block)
    grad_query_proj = query_pull(grad_query)[0]
    grad_key_proj = key_pull(grad_keys)[0]
    grad_value_proj = grad_values.reshape(token_rows, -1)
    grad_projected = jnp.stack([grad_query_proj, grad_key_proj, grad_value_proj], axis=1).astype(
        bfloat
    )
    grad_hidden_one = tensor_sum(
        lambda rows: jnp.einsum("tce,cde->td", rows, qkv_weight, preferred_element_type=float32),
        grad_projected,
    )
    grad_qkv = jnp.einsum(
        "td,tce->ced", hidden_one, grad_projected, preferred_element_type=float32
    )
    gain_grad_one = jnp.einsum("ced,cde->d", grad_qkv, qkv_weight.astype(float32)) / gain_one
    gains = jnp.stack([gain_grad_one, gain_grad_two])
    for mask in (1, 2):
        gains = gains + across(gains, mask)
    mask = 1
    while mask < dp_size:
        gains = gains + swap(gains, "dp", mask, dp_size)
        mask *= 2

    norm_one_pull = jax.vjp(lambda rows: layer_norm(rows, gain_one), layer_mine)[1]
    both_norms = norm_two_part + norm_one_pull(grad_hidden_one)[0]
    input_mine = (cot_mine + both_norms).astype(bfloat)
    input_other = (cot_other + across(both_norms, 1)).astype(bfloat)
    input_grad = place_two(input_mine, input_other, core).reshape(token_rows, width)

    early = dp_sum([grad_up.reshape(2 * units, width), grad_down, grad_out], me, dp_size)
    late = dp_sum([grad_qkv.reshape(3 * columns, width)], me, dp_size)
    grad_up = early[: 2 * units].reshape(2, units, width).transpose(0, 2, 1)
    grad_down = early[2 * units : 3 * units]
    grad_out = early[3 * units :]
    grad_qkv = late.reshape(3, columns, width).transpose(0, 2, 1)
    return (layer_out, input_grad, grad_qkv, grad_out, grad_up, grad_down, gains[0], gains[1])


def solution(mesh):
    return jax.shard_map(
        functools.partial(per_device, mesh.shape["tensor"], mesh.shape["dp"]),
        mesh=mesh,
        in_specs=(
            P("dp", None),
            P("dp"),
            P(None, None, "tensor"),
            P("tensor", None),
            P(None, None, "tensor"),
            P("tensor", None),
            P(),
            P(),
            P("dp", None),
        ),
        out_specs=(
            P("dp", None),
            P("dp", None),
            P(None, None, "tensor"),
            P("tensor", None),
            P(None, None, "tensor"),
            P("tensor", None),
            P(),
            P(),
        ),
        check_vma=False,
    )
```

time: 531 us -> 380 us (0.72)
  waiting for transfers between devices: 389 us -> 197 us
  starting transfers between devices: 0.82 us -> 44.3 us
  blocking collectives: 23.1 us -> 0 us
  other arithmetic: 40.1 us -> 56 us
  between operations: 15.3 us -> 3.33 us
  local copies, waits for them, and re-layouts: 26.5 us -> 36.2 us
    psum x4 -> x0, waiting for transfers between devices: 389 us -> none  [the longest x1 148 us: per_device(): lax.psum((grad_qkv, grad_out, grad_up, grad_down, grad_gain_one, grad_gai...]
    ppermute x0 -> x45, waiting for transfers between devices: none -> 197 us  [swap(): return lax.ppermute(array, axis, [(i, i ^ mask) for i in range(size)])]
    ppermute x0 -> x45, starting transfers between devices: none -> 44.3 us  [swap(): return lax.ppermute(array, axis, [(i, i ^ mask) for i in range(size)])]
    psum x1 -> x0, blocking collectives: 23.1 us -> none  [per_device(): lax.psum((grad_qkv, grad_out, grad_up, grad_down, grad_gain_one, grad_gai...]
    dynamic_update_slice x0 -> x18, other arithmetic: none -> 21.6 us  [the longest x8 8.87 us: place_two(): both = lax.dynamic_update_index_in_dim(both, mine, bit, 0)]
    unnamed x146 -> x153, local copies, waits for them, and re-layouts: 20.6 us -> 13.5 us
    reduce_sum x3 -> x1, other arithmetic: 9 us -> 2.28 us  [layer_norm(): return centred * lax.rsqrt(variance + 1e-05) * gain]
    dot_general x11 -> x14, matrix products: 23.5 us -> 29.3 us  [the longest x2 5.38 us: per_device(): jnp.einsum('tcf,cdf->td', rows, up_weight, preferred_element_type=float32)]
  transfers between devices with their start and end apart: 4 -> 45, of which waited for: 4 -> 21; matrix products, arithmetic and copies ran while one was open for 5% -> 22% of each run, Pallas kernels for 0% -> 0%
where the time goes in v1:
time: 380 us; the launch traced here: 376 us
  waiting for transfers between devices  197 us (52%)
  other arithmetic  56 us (15%)
  starting transfers between devices  44.3 us (12%)
  matrix products  38.9 us (10%)
  local copies, waits for them, and re-layouts  36.2 us (10%)
    ppermute x45, waiting for transfers between devices, swap(): return lax.ppermute(array, axis, [(i, i ^ mask) for i in range(size)])  197 us
    ppermute x45, starting transfers between devices, swap(): return lax.ppermute(array, axis, [(i, i ^ mask) for i in range(size)])  44.3 us
    unnamed x153, local copies, waits for them, and re-layouts  13.5 us
    dynamic_update_slice x8, other arithmetic, place_two(): both = lax.dynamic_update_index_in_dim(both, mine, bit, 0)  8.87 us
  transfers between devices with their start and end apart: 45, of which 21 were waited for; matrix products, arithmetic and copies ran while one was open for 22% of the time, Pallas kernels for 0%

profile of v1, /device:TPU:0, one launch (start us, length us, event | category | flops | bytes accessed | tf_op | source)
XLA Modules:
  0.0 375.5 jit_solution(2128022424686268224)
XLA Ops:
  5.0 1.8 convert_reduce_fusion
  8.7 1.6 slice_bitcast_fusion.4
  14.6 1.9 fusion.97
  23.9 2.4 multiply_bitcast_fusion.1
  28.4 2.6 collective-permute-start.2
  32.3 1.6 collective-permute-start.1
  34.1 1.9 convert_element_type.132
  38.5 23.6 %collective-permute-done.1 = f32[512,192]{0,1:T(8,128)} collective-permute-done((f32[512,192]{0,1:T(8,128)}, f32[512,192]{0,1:T(8,128)}, u32[]{:S(2)}, u32[]{:S(2)}) %collective-permute-start.1) | collective-permute-done | bytes 393248 | tf_op jit(solution)/shard_map/ppermute | solution.py:63
  66.7 2.6 fusion.131
  70.9 1.7 fusion.42
  73.2 2.1 fusion.138
  76.6 2.4 fusion.44
  79.0 2.5 convolution_bitcast_fusion
  81.5 3.0 fusion.73
  85.2 2.0 convolution_bitcast_fusion.2
  87.6 3.1 multiply_reduce_fusion.2
  93.3 1.8 fusion.93
  95.1 18.7 %collective-permute-done.34 = f32[288,768]{1,0:T(8,128)} collective-permute-done((f32[288,768]{1,0:T(8,128)S(1)}, f32[288,768]{1,0:T(8,128)}, u32[]{:S(2)}, u32[]{:S(2)}) %collective-permute-start.34) | collective-permute-done | bytes 884768 | tf_op jit(solution)/shard_map/ppermute | solution.py:63
  117.4 3.4 bitcast_add_fusion.1
  120.8 1.5 collective-permute-start.11
  122.9 4.7 %collective-permute-done.35 = f32[144,768]{1,0:T(8,128)} collective-permute-done((f32[144,768]{1,0:T(8,128)}, f32[144,768]{1,0:T(8,128)}, u32[]{:S(2)}, u32[]{:S(2)}) %collective-permute-start.35) | collective-permute-done | bytes 442400 | tf_op jit(solution)/shard_map/ppermute | solution.py:63
  128.7 2.6 collective-permute-start.36
  131.3 8.8 %collective-permute-done.36 = f32[72,768]{1,0:T(8,128)S(1)} collective-permute-done((f32[72,768]{1,0:T(8,128)S(1)}, f32[72,768]{1,0:T(8,128)S(1)}, u32[]{:S(2)}, u32[]{:S(2)}) %collective-permute-start.36) | collective-permute-done | bytes 221216 | tf_op jit(solution)/shard_map/ppermute | solution.py:63
  140.3 3.2 convolution_add_fusion
  143.5 1.5 collective-permute-start.8
  145.0 7.3 %collective-permute-done.37 = f32[72,768]{1,0:T(8,128)S(1)} collective-permute-done((f32[72,768]{1,0:T(8,128)S(1)}, f32[72,768]{1,0:T(8,128)S(1)}, u32[]{:S(2)}, u32[]{:S(2)}) %collective-permute-start.37) | collective-permute-done | bytes 221216 | tf_op jit(solution)/shard_map/ppermute | solution.py:63
  154.1 4.3 %collective-permute-done.11 = f32[512,768]{1,0:T(8,128)} collective-permute-done((f32[512,768]{1,0:T(8,128)}, f32[512,768]{1,0:T(8,128)}, u32[]{:S(2)}, u32[]{:S(2)}) %collective-permute-start.11) | collective-permute-done | bytes 1572896 | tf_op jit(solution)/shard_map/ppermute | solution.py:63
  158.4 2.3 multiply_reduce_fusion.6
  160.7 2.5 fusion.129
  165.2 1.7 fusion.56
  167.7 1.5 collective-permute-start.39
  169.2 1.5 fusion.139
  172.2 17.8 %collective-permute-done.39 = f32[288,768]{1,0:T(8,128)} collective-permute-done((f32[288,768]{1,0:T(8,128)}, f32[288,768]{1,0:T(8,128)}, u32[]{:S(2)}, u32[]{:S(2)}) %collective-permute-start.39) | collective-permute-done | bytes 884768 | tf_op jit(solution)/shard_map/ppermute | solution.py:63
  192.7 3.6 fusion.46
  196.3 3.0 fusion.52
  199.3 2.2 convolution_convert_fusion
  201.6 1.8 multiply_reduce_fusion
  212.9 1.9 stack_reshape_reshape.4
  214.8 2.7 fusion.62
  219.5 2.0 fusion.126
  222.7 1.5 collective-permute-start.41
  224.2 1.6 collective-permute-start.16
  227.9 1.6 collective-permute-start.22
  229.5 7.9 %collective-permute-done.42 = f32[2,768]{1,0:T(2,128)S(1)} collective-permute-done((f32[2,768]{1,0:T(2,128)S(1)}, f32[2,768]{1,0:T(2,128)S(1)}, u32[]{:S(2)}, u32[]{:S(2)}) %collective-permute-start.42) | collective-permute-done | bytes 6176 | tf_op jit(solution)/shard_map/ppermute | solution.py:63
  237.4 1.6 collective-permute-start.43
  239.8 14.6 %collective-permute-done.43 = f32[2,768]{1,0:T(2,128)S(1)} collective-permute-done((f32[2,768]{1,0:T(2,128)S(1)}, f32[2,768]{1,0:T(2,128)S(1)}, u32[]{:S(2)}, u32[]{:S(2)}) %collective-permute-start.43) | collective-permute-done | bytes 6176 | tf_op jit(solution)/shard_map/ppermute | solution.py:63
  254.5 2.6 collective-permute-start.44
  257.1 1.6 fusion.48
  260.6 2.5 collective-permute-start.23
  263.1 9.9 %collective-permute-done.17 = f32[80,768]{1,0:T(8,128)S(1)} collective-permute-done((f32[80,768]{1,0:T(8,128)S(1)}, f32[80,768]{1,0:T(8,128)S(1)}, u32[]{:S(2)}, u32[]{:S(2)}) %collective-permute-start.17) | collective-permute-done | bytes 245792 | tf_op jit(solution)/shard_map/ppermute | solution.py:63
  273.2 1.6 collective-permute-start.24
  274.7 5.0 %collective-permute-done.18 = f32[40,768]{1,0:T(8,128)S(1)} collective-permute-done((f32[40,768]{1,0:T(8,128)S(1)}, f32[40,768]{1,0:T(8,128)S(1)}, u32[]{:S(2)}, u32[]{:S(2)}) %collective-permute-start.18) | collective-permute-done | bytes 122912 | tf_op jit(solution)/shard_map/ppermute | solution.py:63
  280.0 1.6 collective-permute-start.25
  281.8 3.0 collective-permute-start.29
  284.7 13.1 %collective-permute-done.19 = f32[40,768]{1,0:T(8,128)S(1)} collective-permute-done((f32[40,768]{1,0:T(8,128)S(1)}, f32[40,768]{1,0:T(8,128)S(1)}, u32[]{:S(2)}, u32[]{:S(2)}) %collective-permute-start.19) | collective-permute-done | bytes 122912 | tf_op jit(solution)/shard_map/ppermute | solution.py:63
  298.0 2.2 collective-permute-start.26
  301.1 1.6 collective-permute-start.14
  302.8 9.9 %collective-permute-done.29 = f32[144,768]{1,0:T(8,128)S(1)} collective-permute-done((f32[144,768]{1,0:T(8,128)S(1)}, f32[144,768]{1,0:T(8,128)S(1)}, u32[]{:S(2)}, u32[]{:S(2)}) %collective-permute-start.29) | collective-permute-done | bytes 442400 | tf_op jit(solution)/shard_map/ppermute | solution.py:63
  312.7 1.5 collective-permute-start.30
  314.9 6.2 %collective-permute-done.30 = f32[72,768]{1,0:T(8,128)S(1)} collective-permute-done((f32[72,768]{1,0:T(8,128)S(1)}, f32[72,768]{1,0:T(8,128)S(1)}, u32[]{:S(2)}, u32[]{:S(2)}) %collective-permute-start.30) | collective-permute-done | bytes 221216 | tf_op jit(solution)/shard_map/ppermute | solution.py:63
  322.9 9.8 %collective-permute-done.31 = f32[72,768]{1,0:T(8,128)S(1)} collective-permute-done((f32[72,768]{1,0:T(8,128)S(1)}, f32[72,768]{1,0:T(8,128)S(1)}, u32[]{:S(2)}, u32[]{:S(2)}) %collective-permute-start.31) | collective-permute-done | bytes 221216 | tf_op jit(solution)/shard_map/ppermute | solution.py:63
  335.9 1.7 fusion.54
  337.7 14.0 %collective-permute-done.32 = f32[144,768]{1,0:T(8,128)S(1)} collective-permute-done((f32[144,768]{1,0:T(8,128)S(1)}, f32[144,768]{1,0:T(8,128)S(1)}, u32[]{:S(2)}, u32[]{:S(2)}) %collective-permute-start.32) | collective-permute-done | bytes 442400 | tf_op jit(solution)/shard_map/ppermute | solution.py:63
  353.6 18.5 %collective-permute-done.33 = f32[288,768]{1,0:T(8,128)S(1)} collective-permute-done((f32[288,768]{1,0:T(8,128)S(1)}, f32[288,768]{1,0:T(8,128)S(1)}, u32[]{:S(2)}, u32[]{:S(2)}) %collective-permute-start.33) | collective-permute-done | bytes 884768 | tf_op jit(solution)/shard_map/ppermute | solution.py:63
  (364 shorter events, 78.2 us)
Async XLA Ops:
  0.6 72.6 %copy-start = (bf16[288,768]{1,0:T(8,128)(2,1)S(1)}, bf16[288,768]{1,0:T(8,128)(2,1)}, u32[]{:S(2)}) copy-start(bf16[288,768]{1,0:T(8,128)(2,1)} %param.14) | copy-start | bytes 1327108
  0.6 6.1 %copy-start.5 = (bf16[1024,768]{1,0:T(8,128)(2,1)S(1)}, bf16[1024,768]{1,0:T(8,128)(2,1)}, u32[]{:S(2)}) copy-start(bf16[1024,768]{1,0:T(8,128)(2,1)} %param.9) | copy-start | bytes 4718596
  26.9 4.2 %copy-start.41 = (bf16[192,768]{1,0:T(8,128)(2,1)S(1)}, bf16[192,768]{1,0:T(8,128)(2,1)}, u32[]{:S(2)}) copy-start(bf16[192,768]{1,0:T(8,128)(2,1)} %param.12) | copy-start | bytes 884740
  28.0 9.5 %collective-permute-start = (f32[512,192]{0,1:T(8,128)}, f32[512,192]{0,1:T(8,128)}, u32[]{:S(2)}, u32[]{:S(2)}) collective-permute-start(f32[512,192]{0,1:T(8,128)} %get-tuple-element.54), channel_id=1, source_target_pairs={{0,1},{1,0},{2,3},{3,2},{4,5},{5,4},{6,7},{7,6},{8,9},{9,8},{10,11... | collective-permute-start | bytes 1179656 | tf_op jit(solution)/shard_map/ppermute | solution.py:63
  28.4 34.8 %collective-permute-start.2 = (f32[512,192]{0,1:T(8,128)}, f32[512,192]{0,1:T(8,128)}, u32[]{:S(2)}, u32[]{:S(2)}) collective-permute-start(f32[512,192]{0,1:T(8,128)} %get-tuple-element.54), channel_id=1, source_target_pairs={{0,3},{1,2},{2,1},{3,0},{4,7},{5,6},{6,5},{7,4},{8,11},{9,10},{10,... | collective-permute-start | bytes 1179656 | tf_op jit(solution)/shard_map/ppermute | solution.py:63
  31.9 32.5 %collective-permute-start.3 = (f32[192,768]{1,0:T(8,128)}, f32[192,768]{1,0:T(8,128)}, u32[]{:S(2)}, u32[]{:S(2)}) collective-permute-start(f32[192,768]{1,0:T(8,128)} %convert_multiply_fusion), channel_id=1, source_target_pairs={{0,1},{1,0},{2,3},{3,2},{4,5},{5,4},{6,7},{7,6},{8,9},{9,8},{10,11... | collective-permute-start | bytes 1769480 | tf_op jit(solution)/shard_map/ppermute | solution.py:63
  31.9 31.2 %collective-permute-start.4 = (f32[192,768]{1,0:T(8,128)}, f32[192,768]{1,0:T(8,128)}, u32[]{:S(2)}, u32[]{:S(2)}) collective-permute-start(f32[192,768]{1,0:T(8,128)} %convert_multiply_fusion), channel_id=1, source_target_pairs={{0,2},{1,3},{2,0},{3,1},{4,6},{5,7},{6,4},{7,5},{8,10},{9,11},{10,... | collective-permute-start | bytes 1769480 | tf_op jit(solution)/shard_map/ppermute | solution.py:63
  32.3 29.8 %collective-permute-start.1 = (f32[512,192]{0,1:T(8,128)}, f32[512,192]{0,1:T(8,128)}, u32[]{:S(2)}, u32[]{:S(2)}) collective-permute-start(f32[512,192]{0,1:T(8,128)} %get-tuple-element.53), channel_id=1, source_target_pairs={{0,2},{1,3},{2,0},{3,1},{4,6},{5,7},{6,4},{7,5},{8,10},{9,11},{10,... | collective-permute-start | bytes 1179656 | tf_op jit(solution)/shard_map/ppermute | solution.py:63
  37.3 25.9 %copy-start.14 = (bf16[8,128,3,64]{1,0,3,2:T(8,128)(2,1)}, bf16[8,128,3,64]{1,0,3,2:T(8,128)(2,1)S(1)}, u32[]{:S(2)}) copy-start(bf16[8,128,3,64]{1,0,3,2:T(8,128)(2,1)S(1)} %copy.31) | copy-start | bytes 1179652
  63.2 3.5 collective-permute-start.5
  72.6 4.0 %collective-permute-start.6 = (f32[512,768]{1,0:T(8,128)}, f32[512,768]{1,0:T(8,128)}, u32[]{:S(2)}, u32[]{:S(2)}) collective-permute-start(f32[512,768]{1,0:T(8,128)} %get-tuple-element.33), channel_id=1, source_target_pairs={{0,1},{1,0},{2,3},{3,2},{4,5},{5,4},{6,7},{7,6},{8,9},{9,8},{10,11... | collective-permute-start | bytes 4718600 | tf_op jit(solution)/shard_map/ppermute | solution.py:63
  75.3 3.7 copy-start.46
  87.2 30.2 %collective-permute-start.10 = (f32[512,768]{1,0:T(8,128)}, f32[512,768]{1,0:T(8,128)}, u32[]{:S(2)}, u32[]{:S(2)}) collective-permute-start(f32[512,768]{1,0:T(8,128)} %convolution_bitcast_fusion.2), channel_id=1, source_target_pairs={{0,1},{1,0},{2,3},{3,2},{4,5},{5,4},{6,7},{7,6},{8,9},{9,8},{10,11... | collective-permute-start | bytes 4718600 | tf_op jit(solution)/shard_map/ppermute | solution.py:63
  91.9 21.9 %collective-permute-start.34 = (f32[288,768]{1,0:T(8,128)S(1)}, f32[288,768]{1,0:T(8,128)}, u32[]{:S(2)}, u32[]{:S(2)}) collective-permute-start(f32[288,768]{1,0:T(8,128)S(1)} %constant_dynamic-slice_fusion.2), channel_id=1, source_target_pairs={{0,4},{4,0},{8,12},{12,8},{16,20},{20,16},{24,28},{28,24},{1,5},{5... | collective-permute-start | bytes 2654216 | tf_op jit(solution)/shard_map/ppermute | solution.py:63
  93.3 20.5 %copy-start.31 = (f32[2,288,768]{2,1,0:T(8,128)S(1)}, f32[2,288,768]{2,1,0:T(8,128)}, u32[]{:S(2)}) copy-start(f32[2,288,768]{2,1,0:T(8,128)} %copy-done.30) | copy-start | bytes 5308420
  95.1 22.3 %copy-start.21 = (bf16[1024,1,288]{0,2,1:T(8,128)(2,1)S(1)}, bf16[1024,1,288]{0,2,1:T(8,128)(2,1)}, u32[]{:S(2)}) copy-start(bf16[1024,1,288]{0,2,1:T(8,128)(2,1)} %copy-done.20) | copy-start | bytes 1769476
  95.1 22.3 %copy-start.27 = (bf16[1024,1,288]{0,2,1:T(8,128)(2,1)S(1)}, bf16[1024,1,288]{0,2,1:T(8,128)(2,1)}, u32[]{:S(2)}) copy-start(bf16[1024,1,288]{0,2,1:T(8,128)(2,1)} %copy-done.26) | copy-start | bytes 1769476
  95.1 22.3 %copy-start.47 = (bf16[2,768,288]{1,2,0:T(8,128)(2,1)S(1)}, bf16[2,768,288]{1,2,0:T(8,128)(2,1)}, u32[]{:S(2)}) copy-start(bf16[2,768,288]{1,2,0:T(8,128)(2,1)} %param.13) | copy-start | bytes 2654212
  95.1 45.2 %collective-permute-start.7 = (f32[512,768]{1,0:T(8,128)}, f32[512,768]{1,0:T(8,128)}, u32[]{:S(2)}, u32[]{:S(2)}) collective-permute-start(f32[512,768]{1,0:T(8,128)} %fusion.93), channel_id=1, source_target_pairs={{0,1},{1,0},{2,3},{3,2},{4,5},{5,4},{6,7},{7,6},{8,9},{9,8},{10,11... | collective-permute-start | bytes 4718600 | tf_op jit(solution)/shard_map/ppermute | solution.py:63
  115.9 11.7 %collective-permute-start.35 = (f32[144,768]{1,0:T(8,128)}, f32[144,768]{1,0:T(8,128)}, u32[]{:S(2)}, u32[]{:S(2)}) collective-permute-start(f32[144,768]{1,0:T(8,128)} %constant_dynamic-slice_fusion.1), channel_id=1, source_target_pairs={{0,8},{4,12},{8,0},{12,4},{16,24},{20,28},{24,16},{28,20},{1,9},{5... | collective-permute-start | bytes 1327112 | tf_op jit(solution)/shard_map/ppermute | solution.py:63
  120.8 37.7 %collective-permute-start.11 = (f32[512,768]{1,0:T(8,128)}, f32[512,768]{1,0:T(8,128)}, u32[]{:S(2)}, u32[]{:S(2)}) collective-permute-start(f32[512,768]{1,0:T(8,128)} %bitcast_add_fusion.1), channel_id=1, source_target_pairs={{0,2},{1,3},{2,0},{3,1},{4,6},{5,7},{6,4},{7,5},{8,10},{9,11},{10,... | collective-permute-start | bytes 4718600 | tf_op jit(solution)/shard_map/ppermute | solution.py:63
  128.7 11.4 %collective-permute-start.36 = (f32[72,768]{1,0:T(8,128)S(1)}, f32[72,768]{1,0:T(8,128)S(1)}, u32[]{:S(2)}, u32[]{:S(2)}) collective-permute-start(f32[72,768]{1,0:T(8,128)S(1)} %constant_dynamic-slice_fusion), channel_id=1, source_target_pairs={{0,16},{4,20},{8,24},{12,28},{16,0},{20,4},{24,8},{28,12},{1,17},{... | collective-permute-start | bytes 663560 | tf_op jit(solution)/shard_map/ppermute | solution.py:63
  140.2 12.0 %collective-permute-start.37 = (f32[72,768]{1,0:T(8,128)S(1)}, f32[72,768]{1,0:T(8,128)S(1)}, u32[]{:S(2)}, u32[]{:S(2)}) collective-permute-start(f32[72,768]{1,0:T(8,128)S(1)} %get-tuple-element.13), channel_id=1, source_target_pairs={{0,16},{4,20},{8,24},{12,28},{16,0},{20,4},{24,8},{28,12},{1,17},{... | collective-permute-start | bytes 663560 | tf_op jit(solution)/shard_map/ppermute | solution.py:63
  143.5 47.8 %collective-permute-start.8 = (f32[512,768]{1,0:T(8,128)}, f32[512,768]{1,0:T(8,128)}, u32[]{:S(2)}, u32[]{:S(2)}) collective-permute-start(f32[512,768]{1,0:T(8,128)} %convolution_add_fusion), channel_id=1, source_target_pairs={{0,2},{1,3},{2,0},{3,1},{4,6},{5,7},{6,4},{7,5},{8,10},{9,11},{10,... | collective-permute-start | bytes 4718600 | tf_op jit(solution)/shard_map/ppermute | solution.py:63
  152.2 14.6 %collective-permute-start.38 = (f32[144,768]{1,0:T(8,128)S(1)}, f32[144,768]{1,0:T(8,128)S(1)}, u32[]{:S(2)}, u32[]{:S(2)}) collective-permute-start(f32[144,768]{1,0:T(8,128)S(1)} %bitcast.454), channel_id=1, source_target_pairs={{0,8},{4,12},{8,0},{12,4},{16,24},{20,28},{24,16},{28,20},{1,9},{5... | collective-permute-start | bytes 1327112 | tf_op jit(solution)/shard_map/ppermute | solution.py:63
  154.1 6.6 %copy-start.56 = (f32[512]{0:T(512)S(1)}, f32[512]{0:T(512)}, u32[]{:S(2)}) copy-start(f32[512]{0:T(512)} %copy-done.55) | copy-start | bytes 6148
  165.2 4.0 %copy-start.60 = (f32[512]{0:T(512)S(1)}, f32[512]{0:T(512)}, u32[]{:S(2)}) copy-start(f32[512]{0:T(512)} %get-tuple-element.38) | copy-start | bytes 6148
  165.2 4.0 %copy-start.62 = (bf16[768]{0:T(1024)(128)(2,1)S(1)}, bf16[768]{0:T(1024)(128)(2,1)}, u32[]{:S(2)}) copy-start(bf16[768]{0:T(1024)(128)(2,1)} %param.16) | copy-start | bytes 4612
  165.2 4.0 %copy-start.67 = (f32[768]{0:T(1024)S(1)}, f32[768]{0:T(1024)}, u32[]{:S(2)}) copy-start(f32[768]{0:T(1024)} %get-tuple-element.89) | copy-start | bytes 9220
  166.9 29.4 %collective-permute-start.12 = (f32[512,768]{1,0:T(8,128)}, f32[512,768]{1,0:T(8,128)}, u32[]{:S(2)}, u32[]{:S(2)}) collective-permute-start(f32[512,768]{1,0:T(8,128)} %get-tuple-element.25), channel_id=1, source_target_pairs={{0,1},{1,0},{2,3},{3,2},{4,5},{5,4},{6,7},{7,6},{8,9},{9,8},{10,11... | collective-permute-start | bytes 4718600 | tf_op jit(solution)/shard_map/ppermute | solution.py:63
  167.7 22.4 %collective-permute-start.39 = (f32[288,768]{1,0:T(8,128)}, f32[288,768]{1,0:T(8,128)}, u32[]{:S(2)}, u32[]{:S(2)}) collective-permute-start(f32[288,768]{1,0:T(8,128)} %bitcast.101), channel_id=1, source_target_pairs={{0,4},{4,0},{8,12},{12,8},{16,20},{20,16},{24,28},{28,24},{1,5},{5... | collective-permute-start | bytes 2654216 | tf_op jit(solution)/shard_map/ppermute | solution.py:63
  170.9 21.7 %copy-start.11 = (f32[512,768,1]{1,0,2:T(8,128)S(1)}, f32[512,768,1]{1,0,2:T(8,128)}, u32[]{:S(2)}) copy-start(f32[512,768,1]{1,0,2:T(8,128)} %get-tuple-element.86) | copy-start | bytes 4718596
  172.2 20.4 %copy-start.4 = (f32[1024,768]{1,0:T(8,128)S(1)}, f32[1024,768]{1,0:T(8,128)}, u32[]{:S(2)}) copy-start(f32[1024,768]{1,0:T(8,128)} %convert_element_type.132) | copy-start | bytes 9437188
  192.5 9.0 %slice-start = ((s8[4718592]{0:T(1024)(128)(4,1)}), s8[4194304]{0:T(1024)(128)(4,1)S(1)}, s32[]{:S(2)}) async-start(s8[4718592]{0:T(1024)(128)(4,1)} %bitcast.427), calls=%async_computation | async-start | bytes 8388608
  192.6 3.7 copy-start.8
  192.6 8.9 %slice-start.1 = ((s8[4718592]{0:T(1024)(128)(4,1)}), s8[524288]{0:T(1024)(128)(4,1)S(1)}, s32[]{:S(2)}) async-start(s8[4718592]{0:T(1024)(128)(4,1)} %bitcast.427), calls=%async_computation.1 | async-start | bytes 1048576
  196.3 58.2 %collective-permute-start.9 = (f32[512,768]{1,0:T(8,128)}, f32[512,768]{1,0:T(8,128)}, u32[]{:S(2)}, u32[]{:S(2)}) collective-permute-start(f32[512,768]{1,0:T(8,128)} %get-tuple-element.31), channel_id=1, source_target_pairs={{0,1},{1,0},{2,3},{3,2},{4,5},{5,4},{6,7},{7,6},{8,9},{9,8},{10,11... | collective-permute-start | bytes 4718600 | tf_op jit(solution)/shard_map/ppermute | solution.py:63
  219.4 3.3 collective-permute-start.40
  221.7 59.8 %collective-permute-start.28 = (f32[288,768]{1,0:T(8,128)S(1)}, f32[288,768]{1,0:T(8,128)S(1)}, u32[]{:S(2)}, u32[]{:S(2)}) collective-permute-start(f32[288,768]{1,0:T(8,128)S(1)} %constant_dynamic-slice_fusion.5), channel_id=1, source_target_pairs={{0,8},{4,12},{8,0},{12,4},{16,24},{20,28},{24,16},{28,20},{1,9},{5... | collective-permute-start | bytes 2654216 | tf_op jit(solution)/shard_map/ppermute | solution.py:63
  222.7 3.7 collective-permute-start.41
  224.2 35.6 %collective-permute-start.16 = (f32[160,768]{1,0:T(8,128)S(1)}, f32[160,768]{1,0:T(8,128)S(1)}, u32[]{:S(2)}, u32[]{:S(2)}) collective-permute-start(f32[160,768]{1,0:T(8,128)S(1)} %constant_dynamic-slice_fusion.11), channel_id=1, source_target_pairs={{0,4},{4,0},{8,12},{12,8},{16,20},{20,16},{24,28},{28,24},{1,5},{5... | collective-permute-start | bytes 1474568 | tf_op jit(solution)/shard_map/ppermute | solution.py:63
  226.4 11.0 %collective-permute-start.42 = (f32[2,768]{1,0:T(2,128)S(1)}, f32[2,768]{1,0:T(2,128)S(1)}, u32[]{:S(2)}, u32[]{:S(2)}) collective-permute-start(f32[2,768]{1,0:T(2,128)S(1)} %fusion.165), channel_id=1, source_target_pairs={{0,4},{4,0},{8,12},{12,8},{16,20},{20,16},{24,28},{28,24},{1,5},{5... | collective-permute-start | bytes 18440 | tf_op jit(solution)/shard_map/ppermute | solution.py:63
  227.9 32.6 %collective-permute-start.22 = (f32[160,768]{1,0:T(8,128)S(1)}, f32[160,768]{1,0:T(8,128)S(1)}, u32[]{:S(2)}, u32[]{:S(2)}) collective-permute-start(f32[160,768]{1,0:T(8,128)S(1)} %constant_dynamic-slice_fusion.8), channel_id=1, source_target_pairs={{0,8},{4,12},{8,0},{12,4},{16,24},{20,28},{24,16},{28,20},{1,9},{5... | collective-permute-start | bytes 1474568 | tf_op jit(solution)/shard_map/ppermute | solution.py:63
  237.4 19.7 %copy-start.37 = (bf16[2,512,768]{2,1,0:T(8,128)(2,1)S(1)}, bf16[2,512,768]{2,1,0:T(8,128)(2,1)}, u32[]{:S(2)}) copy-start(bf16[2,512,768]{2,1,0:T(8,128)(2,1)} %copy-done.36) | copy-start | bytes 4718596
  237.4 17.1 %collective-permute-start.43 = (f32[2,768]{1,0:T(2,128)S(1)}, f32[2,768]{1,0:T(2,128)S(1)}, u32[]{:S(2)}, u32[]{:S(2)}) collective-permute-start(f32[2,768]{1,0:T(2,128)S(1)} %add.508), channel_id=1, source_target_pairs={{0,8},{4,12},{8,0},{12,4},{16,24},{20,28},{24,16},{28,20},{1,9},{5... | collective-permute-start | bytes 18440 | tf_op jit(solution)/shard_map/ppermute | solution.py:63
  254.4 45.8 %collective-permute-start.13 = (f32[512,768]{1,0:T(8,128)S(1)}, f32[512,768]{1,0:T(8,128)S(1)}, u32[]{:S(2)}, u32[]{:S(2)}) collective-permute-start(f32[512,768]{1,0:T(8,128)S(1)} %convolution_bitcast_fusion.1), channel_id=1, source_target_pairs={{0,1},{1,0},{2,3},{3,2},{4,5},{5,4},{6,7},{7,6},{8,9},{9,8},{10,11... | collective-permute-start | bytes 4718600 | tf_op jit(solution)/shard_map/ppermute | solution.py:63
  254.5 4.7 %collective-permute-start.44 = (f32[2,768]{1,0:T(2,128)S(1)}, f32[2,768]{1,0:T(2,128)S(1)}, u32[]{:S(2)}, u32[]{:S(2)}) collective-permute-start(f32[2,768]{1,0:T(2,128)S(1)} %add.509), channel_id=1, source_target_pairs={{0,16},{4,20},{8,24},{12,28},{16,0},{20,4},{24,8},{28,12},{1,17},{... | collective-permute-start | bytes 18440 | tf_op jit(solution)/shard_map/ppermute | solution.py:63
  259.9 13.0 %collective-permute-start.17 = (f32[80,768]{1,0:T(8,128)S(1)}, f32[80,768]{1,0:T(8,128)S(1)}, u32[]{:S(2)}, u32[]{:S(2)}) collective-permute-start(f32[80,768]{1,0:T(8,128)S(1)} %constant_dynamic-slice_fusion.10), channel_id=1, source_target_pairs={{0,8},{4,12},{8,0},{12,4},{16,24},{20,28},{24,16},{28,20},{1,9},{5... | collective-permute-start | bytes 737288 | tf_op jit(solution)/shard_map/ppermute | solution.py:63
  260.6 12.5 %collective-permute-start.23 = (f32[80,768]{1,0:T(8,128)S(1)}, f32[80,768]{1,0:T(8,128)S(1)}, u32[]{:S(2)}, u32[]{:S(2)}) collective-permute-start(f32[80,768]{1,0:T(8,128)S(1)} %constant_dynamic-slice_fusion.7), channel_id=1, source_target_pairs={{0,16},{4,20},{8,24},{12,28},{16,0},{20,4},{24,8},{28,12},{1,17},{... | collective-permute-start | bytes 737288 | tf_op jit(solution)/shard_map/ppermute | solution.py:63
  273.0 6.8 %collective-permute-start.18 = (f32[40,768]{1,0:T(8,128)S(1)}, f32[40,768]{1,0:T(8,128)S(1)}, u32[]{:S(2)}, u32[]{:S(2)}) collective-permute-start(f32[40,768]{1,0:T(8,128)S(1)} %constant_dynamic-slice_fusion.9), channel_id=1, source_target_pairs={{0,16},{4,20},{8,24},{12,28},{16,0},{20,4},{24,8},{28,12},{1,17},{... | collective-permute-start | bytes 368648 | tf_op jit(solution)/shard_map/ppermute | solution.py:63
  273.2 6.8 %collective-permute-start.24 = (f32[40,768]{1,0:T(8,128)S(1)}, f32[40,768]{1,0:T(8,128)S(1)}, u32[]{:S(2)}, u32[]{:S(2)}) collective-permute-start(f32[40,768]{1,0:T(8,128)S(1)} %constant_dynamic-slice_fusion.6), channel_id=1, source_target_pairs={{0,4},{4,0},{8,12},{12,8},{16,20},{20,16},{24,28},{28,24},{1,5},{5... | collective-permute-start | bytes 368648 | tf_op jit(solution)/shard_map/ppermute | solution.py:63
  279.8 18.0 %collective-permute-start.19 = (f32[40,768]{1,0:T(8,128)S(1)}, f32[40,768]{1,0:T(8,128)S(1)}, u32[]{:S(2)}, u32[]{:S(2)}) collective-permute-start(f32[40,768]{1,0:T(8,128)S(1)} %get-tuple-element.17), channel_id=1, source_target_pairs={{0,16},{4,20},{8,24},{12,28},{16,0},{20,4},{24,8},{28,12},{1,17},{... | collective-permute-start | bytes 368648 | tf_op jit(solution)/shard_map/ppermute | solution.py:63
  280.0 18.0 %collective-permute-start.25 = (f32[40,768]{1,0:T(8,128)S(1)}, f32[40,768]{1,0:T(8,128)S(1)}, u32[]{:S(2)}, u32[]{:S(2)}) collective-permute-start(f32[40,768]{1,0:T(8,128)S(1)} %get-tuple-element.19), channel_id=1, source_target_pairs={{0,4},{4,0},{8,12},{12,8},{16,20},{20,16},{24,28},{28,24},{1,5},{5... | collective-permute-start | bytes 368648 | tf_op jit(solution)/shard_map/ppermute | solution.py:63
  281.8 30.9 %collective-permute-start.29 = (f32[144,768]{1,0:T(8,128)S(1)}, f32[144,768]{1,0:T(8,128)S(1)}, u32[]{:S(2)}, u32[]{:S(2)}) collective-permute-start(f32[144,768]{1,0:T(8,128)S(1)} %constant_dynamic-slice_fusion.4), channel_id=1, source_target_pairs={{0,16},{4,20},{8,24},{12,28},{16,0},{20,4},{24,8},{28,12},{1,17},{... | collective-permute-start | bytes 1327112 | tf_op jit(solution)/shard_map/ppermute | solution.py:63
  297.9 16.3 %collective-permute-start.20 = (f32[80,768]{1,0:T(8,128)S(1)}, f32[80,768]{1,0:T(8,128)S(1)}, u32[]{:S(2)}, u32[]{:S(2)}) collective-permute-start(f32[80,768]{1,0:T(8,128)S(1)} %bitcast.472), channel_id=1, source_target_pairs={{0,8},{4,12},{8,0},{12,4},{16,24},{20,28},{24,16},{28,20},{1,9},{5... | collective-permute-start | bytes 737288 | tf_op jit(solution)/shard_map/ppermute | solution.py:63
  298.0 24.7 %collective-permute-start.26 = (f32[80,768]{1,0:T(8,128)S(1)}, f32[80,768]{1,0:T(8,128)S(1)}, u32[]{:S(2)}, u32[]{:S(2)}) collective-permute-start(f32[80,768]{1,0:T(8,128)S(1)} %bitcast.474), channel_id=1, source_target_pairs={{0,16},{4,20},{8,24},{12,28},{16,0},{20,4},{24,8},{28,12},{1,17},{... | collective-permute-start | bytes 737288 | tf_op jit(solution)/shard_map/ppermute | solution.py:63
  301.1 32.0 %collective-permute-start.14 = (f32[512,768]{1,0:T(8,128)S(1)}, f32[512,768]{1,0:T(8,128)S(1)}, u32[]{:S(2)}, u32[]{:S(2)}) collective-permute-start(f32[512,768]{1,0:T(8,128)S(1)} %bitcast_add_fusion), channel_id=1, source_target_pairs={{0,2},{1,3},{2,0},{3,1},{4,6},{5,7},{6,4},{7,5},{8,10},{9,11},{10,... | collective-permute-start | bytes 4718600 | tf_op jit(solution)/shard_map/ppermute | solution.py:63
  312.7 8.4 %collective-permute-start.30 = (f32[72,768]{1,0:T(8,128)S(1)}, f32[72,768]{1,0:T(8,128)S(1)}, u32[]{:S(2)}, u32[]{:S(2)}) collective-permute-start(f32[72,768]{1,0:T(8,128)S(1)} %constant_dynamic-slice_fusion.3), channel_id=1, source_target_pairs={{0,4},{4,0},{8,12},{12,8},{16,20},{20,16},{24,28},{28,24},{1,5},{5... | collective-permute-start | bytes 663560 | tf_op jit(solution)/shard_map/ppermute | solution.py:63
  314.2 37.8 %collective-permute-start.21 = (f32[160,768]{1,0:T(8,128)S(1)}, f32[160,768]{1,0:T(8,128)S(1)}, u32[]{:S(2)}, u32[]{:S(2)}) collective-permute-start(f32[160,768]{1,0:T(8,128)S(1)} %bitcast.447), channel_id=1, source_target_pairs={{0,4},{4,0},{8,12},{12,8},{16,20},{20,16},{24,28},{28,24},{1,5},{5... | collective-permute-start | bytes 1474568 | tf_op jit(solution)/shard_map/ppermute | solution.py:63
  321.3 11.5 %collective-permute-start.31 = (f32[72,768]{1,0:T(8,128)S(1)}, f32[72,768]{1,0:T(8,128)S(1)}, u32[]{:S(2)}, u32[]{:S(2)}) collective-permute-start(f32[72,768]{1,0:T(8,128)S(1)} %get-tuple-element.15), channel_id=1, source_target_pairs={{0,4},{4,0},{8,12},{12,8},{16,20},{20,16},{24,28},{28,24},{1,5},{5... | collective-permute-start | bytes 663560 | tf_op jit(solution)/shard_map/ppermute | solution.py:63
  322.7 29.3 %collective-permute-start.27 = (f32[160,768]{1,0:T(8,128)S(1)}, f32[160,768]{1,0:T(8,128)S(1)}, u32[]{:S(2)}, u32[]{:S(2)}) collective-permute-start(f32[160,768]{1,0:T(8,128)S(1)} %bitcast.449), channel_id=1, source_target_pairs={{0,8},{4,12},{8,0},{12,4},{16,24},{20,28},{24,16},{28,20},{1,9},{5... | collective-permute-start | bytes 1474568 | tf_op jit(solution)/shard_map/ppermute | solution.py:63
  332.8 19.0 %collective-permute-start.32 = (f32[144,768]{1,0:T(8,128)S(1)}, f32[144,768]{1,0:T(8,128)S(1)}, u32[]{:S(2)}, u32[]{:S(2)}) collective-permute-start(f32[144,768]{1,0:T(8,128)S(1)} %bitcast.456), channel_id=1, source_target_pairs={{0,16},{4,20},{8,24},{12,28},{16,0},{20,4},{24,8},{28,12},{1,17},{... | collective-permute-start | bytes 1327112 | tf_op jit(solution)/shard_map/ppermute | solution.py:63
  337.7 36.3 %collective-permute-start.15 = (f32[512,768]{1,0:T(8,128)S(1)}, f32[512,768]{1,0:T(8,128)S(1)}, u32[]{:S(2)}, u32[]{:S(2)}) collective-permute-start(f32[512,768]{1,0:T(8,128)S(1)} %get-tuple-element.21), channel_id=1, source_target_pairs={{0,1},{1,0},{2,3},{3,2},{4,5},{5,4},{6,7},{7,6},{8,9},{9,8},{10,11... | collective-permute-start | bytes 4718600 | tf_op jit(solution)/shard_map/ppermute | solution.py:63
  351.8 20.3 %collective-permute-start.33 = (f32[288,768]{1,0:T(8,128)S(1)}, f32[288,768]{1,0:T(8,128)S(1)}, u32[]{:S(2)}, u32[]{:S(2)}) collective-permute-start(f32[288,768]{1,0:T(8,128)S(1)} %bitcast.437), channel_id=1, source_target_pairs={{0,8},{4,12},{8,0},{12,4},{16,24},{20,28},{24,16},{28,20},{1,9},{5... | collective-permute-start | bytes 2654216 | tf_op jit(solution)/shard_map/ppermute | solution.py:63
  (51 other events, 100.0 us)

commit v2 on v1

--- a/solution.py
+++ b/solution.py
@@ -75,38 +75,6 @@
     both = jnp.zeros((2,) + mine.shape, mine.dtype)
     both = lax.dynamic_update_index_in_dim(both, mine, bit, 0)
     return lax.dynamic_update_index_in_dim(both, other, 1 - bit, 0)
-
-
-def halving_sum(buffer, me, masks, size):
-    for mask in masks:
-        bit = (me // mask) % 2
-        half = buffer.shape[0] // 2
-        sent = rows_of(buffer, 1 - bit, half)
-        kept = rows_of(buffer, bit, half)
-        buffer = kept + swap(sent, "dp", mask, size)
-    for mask in reversed(masks):
-        bit = (me // mask) % 2
-        other = swap(buffer, "dp", mask, size)
-        buffer = place_two(buffer, other, bit).reshape((-1,) + buffer.shape[1:])
-    return buffer
-
-
-def dp_sum(pieces, me, size):
-    rows = sum(piece.shape[0] for piece in pieces)
-    unit = 16 * size
-    padded = -(-rows // unit) * unit
-    if padded > rows:
-        pieces = list(pieces) + [jnp.zeros((padded - rows, pieces[0].shape[1]), jnp.float32)]
-    whole = jnp.concatenate(pieces, axis=0)
-    masks = []
-    mask = 1
-    while mask < size:
-        masks.append(mask)
-        mask *= 2
-    cut = padded // 2
-    first = halving_sum(whole[:cut], me, masks, size)
-    second = halving_sum(whole[cut:], me, masks[1:] + masks[:1], size)
-    return jnp.concatenate([first, second], axis=0)[:rows]
 
 
 def per_device(
@@ -254,7 +222,6 @@
 
     grad_down = jnp.einsum("tf,td->fd", activated, out_cotangent, preferred_element_type=float32)
     grad_up = jnp.einsum("td,tcf->cfd", hidden_two, grad_up_parts, preferred_element_type=float32)
-    units = grad_down.shape[0]
     gain_grad_two = jnp.einsum("cfd,cdf->d", grad_up, up_weight.astype(float32)) / gain_two
 
     grad_out = jnp.einsum("te,td->ed", attended, grad_branch, preferred_element_type=float32)
@@ -308,12 +275,13 @@
     input_other = (cot_other + across(both_norms, 1)).astype(bfloat)
     input_grad = place_two(input_mine, input_other, core).reshape(token_rows, width)
 
-    early = dp_sum([grad_up.reshape(2 * units, width), grad_down, grad_out], me, dp_size)
-    late = dp_sum([grad_qkv.reshape(3 * columns, width)], me, dp_size)
-    grad_up = early[: 2 * units].reshape(2, units, width).transpose(0, 2, 1)
-    grad_down = early[2 * units : 3 * units]
-    grad_out = early[3 * units :]
-    grad_qkv = late.reshape(3, columns, width).transpose(0, 2, 1)
+    grad_up, grad_down = lax.psum((grad_up, grad_down), "dp")
+    grad_qkv, grad_out, grad_up, grad_down = lax.optimization_barrier(
+        (grad_qkv, grad_out, grad_up, grad_down)
+    )
+    grad_qkv, grad_out = lax.psum((grad_qkv, grad_out), "dp")
+    grad_up = grad_up.transpose(0, 2, 1)
+    grad_qkv = grad_qkv.transpose(0, 2, 1)
     return (layer_out, input_grad, grad_qkv, grad_out, grad_up, grad_down, gains[0], gains[1])
 
 

time: 380 us -> 414 us (1.089)
  waiting for transfers between devices: 197 us -> 262 us
  starting transfers between devices: 44.3 us -> 16.3 us
  between operations: 3.33 us -> 15.9 us
  other arithmetic: 56 us -> 47.5 us
    psum x0 -> x2, waiting for transfers between devices: none -> 155 us  [the longest x1 81.7 us: per_device(): grad_qkv, grad_out = lax.psum((grad_qkv, grad_out), 'dp')]
    ppermute x45 -> x21, waiting for transfers between devices: 197 us -> 106 us  [swap(): return lax.ppermute(array, axis, [(i, i ^ mask) for i in range(size)])]
    ppermute x45 -> x21, starting transfers between devices: 44.3 us -> 16.3 us  [swap(): return lax.ppermute(array, axis, [(i, i ^ mask) for i in range(size)])]
    unnamed x153 -> x149, local copies, waits for them, and re-layouts: 13.5 us -> 20.6 us
    dynamic_update_slice x20 -> x0, local copies, waits for them, and re-layouts: 4.67 us -> none  [the longest x8 2.38 us: place_two(): both = lax.dynamic_update_index_in_dim(both, mine, bit, 0)]
    dynamic_update_slice x8 -> x4, other arithmetic: 8.87 us -> 6.79 us  [place_two(): both = lax.dynamic_update_index_in_dim(both, mine, bit, 0)]
  transfers between devices with their start and end apart: 45 -> 23, of which waited for: 21 -> 13; matrix products, arithmetic and copies ran while one was open for 22% -> 15% of each run, Pallas kernels for 0% -> 0%
where the time goes in v2:
time: 414 us; the launch traced here: 413 us
  waiting for transfers between devices  262 us (63%)
  other arithmetic  47.5 us (11%)
  matrix products  38.7 us (9%)
  local copies, waits for them, and re-layouts  33.3 us (8%)
  starting transfers between devices  16.3 us (4%)
  between operations  15.9 us (4%)
    ppermute x21, waiting for transfers between devices, swap(): return lax.ppermute(array, axis, [(i, i ^ mask) for i in range(size)])  106 us
    psum x1, waiting for transfers between devices, per_device(): grad_qkv, grad_out = lax.psum((grad_qkv, grad_out), 'dp')  81.7 us
    psum x1, waiting for transfers between devices, per_device(): grad_up, grad_down = lax.psum((grad_up, grad_down), 'dp')  73.6 us
    unnamed x149, local copies, waits for them, and re-layouts  20.6 us
    ppermute x21, starting transfers between devices, swap(): return lax.ppermute(array, axis, [(i, i ^ mask) for i in range(size)])  16.3 us
  transfers between devices with their start and end apart: 23, of which 13 were waited for; matrix products, arithmetic and copies ran while one was open for 15% of the time, Pallas kernels for 0%

profile of v2, /device:TPU:0, one launch (start us, length us, event | category | flops | bytes accessed | tf_op | source)
XLA Modules:
  0.0 413.3 jit_solution(4586101153335698196)
XLA Ops:
  7.2 1.3 slice.134
  11.5 1.8 convert_reduce_fusion
  14.0 1.3 fusion.127
  15.3 1.6 slice_bitcast_fusion.3
  19.1 1.1 fusion.99
  21.2 1.9 fusion.97
  27.1 1.1 fusion.136
  28.3 1.2 fusion
  30.4 2.4 multiply_bitcast_fusion.1
  34.8 2.6 collective-permute-start.2
  38.7 1.6 collective-permute-start.1
  40.5 1.9 convert_element_type.132
  42.3 1.3 copy.31
  45.6 22.9 %collective-permute-done.1 = f32[512,192]{0,1:T(8,128)} collective-permute-done((f32[512,192]{0,1:T(8,128)}, f32[512,192]{0,1:T(8,128)}, u32[]{:S(2)}, u32[]{:S(2)}) %collective-permute-start.1) | collective-permute-done | bytes 393248 | tf_op jit(solution)/shard_map/ppermute | solution.py:63
  69.7 1.2 fusion.107
  73.1 2.0 fusion.131
  75.5 1.3 broadcast.277.clone.1
  76.7 1.7 fusion.42
  79.0 2.1 fusion.137
  81.1 1.3 collective-permute-done.6
  82.4 2.4 fusion.44
  84.8 2.5 convolution_bitcast_fusion
  87.3 2.8 fusion.73
  92.1 3.0 collective-permute-done.10
  96.0 1.4 collective-permute-start.11
  97.5 35.3 %collective-permute-done.11 = f32[512,768]{1,0:T(8,128)S(1)} collective-permute-done((f32[512,768]{1,0:T(8,128)S(1)}, f32[512,768]{1,0:T(8,128)S(1)}, u32[]{:S(2)}, u32[]{:S(2)}) %collective-permute-start.11) | collective-permute-done | bytes 1572896 | tf_op jit(solution)/shard_map/ppermute | solution.py:63
  134.1 1.3 copy-done.7
  135.8 1.8 fusion.93
  139.4 1.1 copy-done.10
  141.3 1.8 multiply_reduce_fusion
  145.5 1.2 fusion.19
  146.7 1.5 fusion.6
  149.3 1.4 bitcast_multiply_fusion.6
  151.9 2.0 stack_reshape_reshape.4
  153.9 1.3 fusion.134
  155.5 1.6 fusion.62
  157.3 1.3 copy-done.49
  158.6 2.0 convolution_bitcast_fusion.1
  160.7 3.7 multiply_reduce_fusion.2
  164.4 3.2 convolution_add_fusion
  167.6 1.4 collective-permute-start.8
  169.0 1.5 fusion.138
  170.6 3.8 bitcast_add_fusion
  175.1 30.0 %collective-permute-done.8 = f32[512,768]{1,0:T(8,128)} collective-permute-done((f32[512,768]{1,0:T(8,128)}, f32[512,768]{1,0:T(8,128)}, u32[]{:S(2)}, u32[]{:S(2)}) %collective-permute-start.8) | collective-permute-done | bytes 1572896 | tf_op jit(solution)/shard_map/ppermute | solution.py:63
  205.3 3.6 fusion.46
  209.0 1.3 fusion.126
  211.3 2.5 multiply_reduce_fusion.3
  213.8 73.6 %all-reduce.18.cloned.1.call-done = (f32[2,288,768]{2,1,0:T(8,128)}, f32[288,768]{1,0:T(8,128)}) async-done(((f32[2,288,768]{2,1,0:T(8,128)}, f32[288,768]{1,0:T(8,128)}), (f32[2,288,768]{2,1,0:T(8,128)}, f32[288,768]{1,0:T(8,128)})) %all-reduce.18.cloned.1.call-update) | async-done | bytes 2654224 | tf_op jit(solution)/shard_map/psum | solution.py:278
  287.5 3.0 multiply_reduce_fusion.5
  290.7 2.6 fusion.128
  293.3 1.2 broadcast.277.clone.2
  295.3 1.2 fusion.54
  297.2 2.8 collective-permute-done.16
  300.0 1.5 collective-permute-start.17
  301.5 2.2 collective-permute-done.17
  303.7 1.5 collective-permute-start.18
  305.2 2.2 collective-permute-done.18
  308.0 3.3 collective-permute-done.19
  311.3 1.5 collective-permute-start.20
  312.9 1.7 fusion.48
  314.6 2.1 collective-permute-done.20
  318.4 81.7 %all-reduce.16.cloned.1.call-done = (f32[3,768,192]{1,2,0:T(8,128)}, f32[192,768]{1,0:T(8,128)}) async-done(((f32[3,768,192]{1,2,0:T(8,128)}, f32[192,768]{1,0:T(8,128)}), (f32[3,768,192]{1,2,0:T(8,128)}, f32[192,768]{1,0:T(8,128)})) %all-reduce.16.cloned.1.call-update) | async-done | bytes 2359312 | tf_op jit(solution)/shard_map/psum | solution.py:282
  400.0 2.9 copy.112
  403.8 1.2 copy.114
  (255 shorter events, 40.7 us)
Async XLA Ops:
  7.2 71.9 %copy-start = (bf16[288,768]{1,0:T(8,128)(2,1)S(1)}, bf16[288,768]{1,0:T(8,128)(2,1)}, u32[]{:S(2)}) copy-start(bf16[288,768]{1,0:T(8,128)(2,1)} %param.14) | copy-start | bytes 1327108
  7.2 6.1 %copy-start.5 = (bf16[1024,768]{1,0:T(8,128)(2,1)S(1)}, bf16[1024,768]{1,0:T(8,128)(2,1)}, u32[]{:S(2)}) copy-start(bf16[1024,768]{1,0:T(8,128)(2,1)} %param.9) | copy-start | bytes 4718596
  7.2 280.2 %all-reduce.18.cloned.1.call-start = ((), (), s32[]{:S(2)}) async-start(), calls=%async_computation.1 | async-start | bytes 5308416 | tf_op jit(solution)/shard_map/psum | solution.py:278
  11.5 2.4 copy-start.63
  11.5 2.4 copy-start.48
  21.1 2.3 copy-start.17
  28.3 2.1 copy-start.1
  30.4 2.4 copy-start.32
  33.3 4.2 %copy-start.47 = (bf16[192,768]{1,0:T(8,128)(2,1)S(1)}, bf16[192,768]{1,0:T(8,128)(2,1)}, u32[]{:S(2)}) copy-start(bf16[192,768]{1,0:T(8,128)(2,1)} %param.12) | copy-start | bytes 884740
  34.4 10.2 %collective-permute-start = (f32[512,192]{0,1:T(8,128)}, f32[512,192]{0,1:T(8,128)}, u32[]{:S(2)}, u32[]{:S(2)}) collective-permute-start(f32[512,192]{0,1:T(8,128)} %get-tuple-element.56), channel_id=1, source_target_pairs={{0,1},{1,0},{2,3},{3,2},{4,5},{5,4},{6,7},{7,6},{8,9},{9,8},{10,11... | collective-permute-start | bytes 1179656 | tf_op jit(solution)/shard_map/ppermute | solution.py:63
  34.8 34.8 %collective-permute-start.2 = (f32[512,192]{0,1:T(8,128)}, f32[512,192]{0,1:T(8,128)}, u32[]{:S(2)}, u32[]{:S(2)}) collective-permute-start(f32[512,192]{0,1:T(8,128)} %get-tuple-element.56), channel_id=1, source_target_pairs={{0,3},{1,2},{2,1},{3,0},{4,7},{5,6},{6,5},{7,4},{8,11},{9,10},{10,... | collective-permute-start | bytes 1179656 | tf_op jit(solution)/shard_map/ppermute | solution.py:63
  38.3 32.5 %collective-permute-start.3 = (f32[192,768]{1,0:T(8,128)}, f32[192,768]{1,0:T(8,128)}, u32[]{:S(2)}, u32[]{:S(2)}) collective-permute-start(f32[192,768]{1,0:T(8,128)} %convert_multiply_fusion), channel_id=1, source_target_pairs={{0,1},{1,0},{2,3},{3,2},{4,5},{5,4},{6,7},{7,6},{8,9},{9,8},{10,11... | collective-permute-start | bytes 1769480 | tf_op jit(solution)/shard_map/ppermute | solution.py:63
  38.3 31.2 %collective-permute-start.4 = (f32[192,768]{1,0:T(8,128)}, f32[192,768]{1,0:T(8,128)}, u32[]{:S(2)}, u32[]{:S(2)}) collective-permute-start(f32[192,768]{1,0:T(8,128)} %convert_multiply_fusion), channel_id=1, source_target_pairs={{0,2},{1,3},{2,0},{3,1},{4,6},{5,7},{6,4},{7,5},{8,10},{9,11},{10,... | collective-permute-start | bytes 1769480 | tf_op jit(solution)/shard_map/ppermute | solution.py:63
  38.7 29.8 %collective-permute-start.1 = (f32[512,192]{0,1:T(8,128)}, f32[512,192]{0,1:T(8,128)}, u32[]{:S(2)}, u32[]{:S(2)}) collective-permute-start(f32[512,192]{0,1:T(8,128)} %get-tuple-element.55), channel_id=1, source_target_pairs={{0,2},{1,3},{2,0},{3,1},{4,6},{5,7},{6,4},{7,5},{8,10},{9,11},{10,... | collective-permute-start | bytes 1179656 | tf_op jit(solution)/shard_map/ppermute | solution.py:63
  42.3 2.1 copy-start.62
  69.6 3.6 copy-start.2
  69.6 3.5 collective-permute-start.5
  78.4 4.0 collective-permute-start.6
  81.1 3.7 copy-start.52
  90.2 5.0 %copy-start.30 = (bf16[1024,1,288]{0,2,1:T(8,128)(2,1)}, bf16[1024,1,288]{0,2,1:T(8,128)(2,1)S(1)}, u32[]{:S(2)}) copy-start(bf16[1024,1,288]{0,2,1:T(8,128)(2,1)S(1)} %get-tuple-element.32) | copy-start | bytes 1769476
  90.8 4.3 %copy-start.24 = (bf16[1024,1,288]{0,2,1:T(8,128)(2,1)}, bf16[1024,1,288]{0,2,1:T(8,128)(2,1)S(1)}, u32[]{:S(2)}) copy-start(bf16[1024,1,288]{0,2,1:T(8,128)(2,1)S(1)} %get-tuple-element.40) | copy-start | bytes 1769476
  90.8 44.9 %copy-start.22 = (bf16[1024,288]{0,1:T(8,128)(2,1)}, bf16[1024,288]{0,1:T(8,128)(2,1)S(1)}, u32[]{:S(2)}) copy-start(bf16[1024,288]{0,1:T(8,128)(2,1)S(1)} %get-tuple-element.41) | copy-start | bytes 1769476
  91.7 3.5 collective-permute-start.10
  96.0 36.7 %collective-permute-start.11 = (f32[512,768]{1,0:T(8,128)S(1)}, f32[512,768]{1,0:T(8,128)S(1)}, u32[]{:S(2)}, u32[]{:S(2)}) collective-permute-start(f32[512,768]{1,0:T(8,128)S(1)} %bitcast_add_fusion.1), channel_id=1, source_target_pairs={{0,2},{1,3},{2,0},{3,1},{4,6},{5,7},{6,4},{7,5},{8,10},{9,11},{10,... | collective-permute-start | bytes 4718600 | tf_op jit(solution)/shard_map/ppermute | solution.py:63
  135.4 5.8 %slice-start = ((s8[4718592]{0:T(1024)(128)(4,1)}), s8[4194304]{0:T(1024)(128)(4,1)S(1)}, s32[]{:S(2)}) async-start(s8[4718592]{0:T(1024)(128)(4,1)} %bitcast.354), calls=%async_computation.2 | async-start | bytes 8388608
  135.7 3.7 copy-start.12
  135.7 3.5 collective-permute-start.12
  135.8 5.4 %slice-start.1 = ((s8[4718592]{0:T(1024)(128)(4,1)}), s8[524288]{0:T(1024)(128)(4,1)S(1)}, s32[]{:S(2)}) async-start(s8[4718592]{0:T(1024)(128)(4,1)} %bitcast.354), calls=%async_computation.3 | async-start | bytes 1048576
  137.6 26.9 %collective-permute-start.7 = (f32[512,768]{1,0:T(8,128)}, f32[512,768]{1,0:T(8,128)}, u32[]{:S(2)}, u32[]{:S(2)}) collective-permute-start(f32[512,768]{1,0:T(8,128)} %fusion.93), channel_id=1, source_target_pairs={{0,1},{1,0},{2,3},{3,2},{4,5},{5,4},{6,7},{7,6},{8,9},{9,8},{10,11... | collective-permute-start | bytes 4718600 | tf_op jit(solution)/shard_map/ppermute | solution.py:63
  139.4 1.8 copy-start.33
  145.5 3.1 copy-start.8
  146.7 1.9 copy-start.20
  157.1 3.5 copy-start.43
  157.1 3.5 copy-start.45
  158.6 2.1 copy-start.25
  158.6 2.1 copy-start.31
  158.6 2.1 copy-start.53
  160.6 3.9 copy-start.23
  160.6 10.0 %collective-permute-start.13 = (f32[512,768]{1,0:T(8,128)}, f32[512,768]{1,0:T(8,128)}, u32[]{:S(2)}, u32[]{:S(2)}) collective-permute-start(f32[512,768]{1,0:T(8,128)} %convolution_bitcast_fusion.1), channel_id=1, source_target_pairs={{0,1},{1,0},{2,3},{3,2},{4,5},{5,4},{6,7},{7,6},{8,9},{9,8},{10,11... | collective-permute-start | bytes 4718600 | tf_op jit(solution)/shard_map/ppermute | solution.py:63
  167.6 37.5 %collective-permute-start.8 = (f32[512,768]{1,0:T(8,128)}, f32[512,768]{1,0:T(8,128)}, u32[]{:S(2)}, u32[]{:S(2)}) collective-permute-start(f32[512,768]{1,0:T(8,128)} %convolution_add_fusion), channel_id=1, source_target_pairs={{0,2},{1,3},{2,0},{3,1},{4,6},{5,7},{6,4},{7,5},{8,10},{9,11},{10,... | collective-permute-start | bytes 4718600 | tf_op jit(solution)/shard_map/ppermute | solution.py:63
  170.5 229.5 %all-reduce.16.cloned.1.call-start = ((), (), s32[]{:S(2)}) async-start(), calls=%async_computation | async-start | bytes 4718592 | tf_op jit(solution)/shard_map/psum | solution.py:282
  170.6 34.7 %copy-start.3 = (f32[1024,768]{1,0:T(8,128)S(1)}, f32[1024,768]{1,0:T(8,128)}, u32[]{:S(2)}) copy-start(f32[1024,768]{1,0:T(8,128)} %convert_element_type.132) | copy-start | bytes 9437188
  174.4 30.8 %copy-start.9 = (f32[512,768,1]{1,0,2:T(8,128)S(1)}, f32[512,768,1]{1,0,2:T(8,128)}, u32[]{:S(2)}) copy-start(f32[512,768,1]{1,0,2:T(8,128)} %get-tuple-element.88) | copy-start | bytes 4718596
  174.4 113.0 %collective-permute-start.14 = (f32[512,768]{1,0:T(8,128)}, f32[512,768]{1,0:T(8,128)}, u32[]{:S(2)}, u32[]{:S(2)}) collective-permute-start(f32[512,768]{1,0:T(8,128)} %bitcast_add_fusion), channel_id=1, source_target_pairs={{0,2},{1,3},{2,0},{3,1},{4,6},{5,7},{6,4},{7,5},{8,10},{9,11},{10,... | collective-permute-start | bytes 4718600 | tf_op jit(solution)/shard_map/ppermute | solution.py:63
  205.3 3.8 copy-start.11
  205.3 3.8 copy-start.15
  205.3 5.1 %copy-start.46 = (bf16[1024,3,64]{0,2,1:T(8,128)(2,1)S(1)}, bf16[1024,3,64]{0,2,1:T(8,128)(2,1)}, u32[]{:S(2)}) copy-start(bf16[1024,3,64]{0,2,1:T(8,128)(2,1)} %copy-done.45) | copy-start | bytes 1179652
  205.3 5.0 %copy-start.50 = (bf16[3,768,192]{1,2,0:T(8,128)(2,1)S(1)}, bf16[3,768,192]{1,2,0:T(8,128)(2,1)}, u32[]{:S(2)}) copy-start(bf16[3,768,192]{1,2,0:T(8,128)(2,1)} %param.11) | copy-start | bytes 2654212
  208.9 2.2 copy-start.6
  208.9 2.2 copy-start.41
  208.9 2.4 copy-start.44
  208.9 103.9 %collective-permute-start.9 = (f32[512,768]{1,0:T(8,128)}, f32[512,768]{1,0:T(8,128)}, u32[]{:S(2)}, u32[]{:S(2)}) collective-permute-start(f32[512,768]{1,0:T(8,128)} %get-tuple-element.35), channel_id=1, source_target_pairs={{0,1},{1,0},{2,3},{3,2},{4,5},{5,4},{6,7},{7,6},{8,9},{9,8},{10,11... | collective-permute-start | bytes 4718600 | tf_op jit(solution)/shard_map/ppermute | solution.py:63
  287.4 3.3 copy-start.4
  293.3 2.0 copy-start.13
  295.3 17.6 %copy-start.38 = (bf16[2,512,768]{2,1,0:T(8,128)(2,1)S(1)}, bf16[2,512,768]{2,1,0:T(8,128)(2,1)}, u32[]{:S(2)}) copy-start(bf16[2,512,768]{2,1,0:T(8,128)(2,1)} %copy-done.37) | copy-start | bytes 4718596
  296.5 20.8 %collective-permute-start.15 = (f32[512,768]{1,0:T(8,128)S(1)}, f32[512,768]{1,0:T(8,128)S(1)}, u32[]{:S(2)}, u32[]{:S(2)}) collective-permute-start(f32[512,768]{1,0:T(8,128)S(1)} %get-tuple-element.25), channel_id=1, source_target_pairs={{0,1},{1,0},{2,3},{3,2},{4,5},{5,4},{6,7},{7,6},{8,9},{9,8},{10,11... | collective-permute-start | bytes 4718600 | tf_op jit(solution)/shard_map/ppermute | solution.py:63
  296.6 3.4 collective-permute-start.16
  300.0 3.7 collective-permute-start.17
  303.7 3.7 collective-permute-start.18
  307.4 3.9 collective-permute-start.19
  311.3 5.3 %collective-permute-start.20 = (f32[2,768]{1,0:T(2,128)S(1)}, f32[2,768]{1,0:T(2,128)S(1)}, u32[]{:S(2)}, u32[]{:S(2)}) collective-permute-start(f32[2,768]{1,0:T(2,128)S(1)} %add.284), channel_id=1, source_target_pairs={{0,16},{4,20},{8,24},{12,28},{16,0},{20,4},{24,8},{28,12},{1,17},{... | collective-permute-start | bytes 18440 | tf_op jit(solution)/shard_map/ppermute | solution.py:63
  314.5 2.7 copy-start.39
  400.0 3.0 copy-start.54
  400.0 3.8 copy-start.34
  (25 other events, 31.4 us)
Sparse Core Ops, SparseCore 0:
  170.6 116.7 all-reduce.17
  291.6 108.3 all-reduce.15

commit v3 on v2

--- a/solution.py
+++ b/solution.py
@@ -3,6 +3,8 @@
 import jax
 import jax.numpy as jnp
 from jax import lax
+from jax.experimental import pallas as pl
+from jax.experimental.pallas import tpu as pltpu
 from jax.sharding import PartitionSpec as P
 
 HD = 64
@@ -75,6 +77,161 @@
     both = jnp.zeros((2,) + mine.shape, mine.dtype)
     both = lax.dynamic_update_index_in_dim(both, mine, bit, 0)
     return lax.dynamic_update_index_in_dim(both, other, 1 - bit, 0)
+
+
+def masks_of(size):
+    masks = []
+    mask = 1
+    while mask < size:
+        masks.append(mask)
+        mask *= 2
+    return masks
+
+
+def late_kernel(dp_size, whole, gains, summed, gain_sum, kept, landed, gain_held, gain_landed, *sems):
+    send_sem, recv_sem, back_send, back_recv, gain_send, gain_recv = sems
+    me = lax.axis_index("dp")
+    lane = lax.axis_index("tensor")
+    masks = masks_of(dp_size)
+    steps = len(masks)
+    rows = whole.shape[0]
+    half = rows // 2
+    orders = (masks, masks[1:] + masks[:1])
+    hops = [("tensor", 1), ("tensor", 2)] + [("dp", mask) for mask in masks]
+
+    def flip(axis, mask):
+        at = me if axis == "dp" else lane
+        bit = (at // mask) % 2
+        return {axis: at + mask * (1 - 2 * bit)}
+
+    barrier = pltpu.get_barrier_semaphore()
+    for axis, mask in hops:
+        pl.semaphore_signal(
+            barrier, inc=1, device_id=flip(axis, mask), device_id_type=pl.DeviceIdType.MESH
+        )
+    pl.semaphore_wait(barrier, len(hops))
+
+    def span(start, size):
+        return pl.ds(pl.multiple_of(start, 8), size)
+
+    def gain_copy(step):
+        return pltpu.make_async_remote_copy(
+            src_ref=gain_held.at[step],
+            dst_ref=gain_landed.at[step],
+            send_sem=gain_send.at[step],
+            recv_sem=gain_recv.at[step],
+            device_id=flip(*hops[step]),
+            device_id_type=pl.DeviceIdType.MESH,
+        )
+
+    def out_copy(chain, step, start, size):
+        mask = orders[chain][step]
+        bit = (me // mask) % 2
+        base = chain * half + half - 2 * size
+        source = whole if step == 0 else kept
+        return pltpu.make_async_remote_copy(
+            src_ref=source.at[span(start + (1 - bit) * size, size)],
+            dst_ref=landed.at[pl.ds(base, size)],
+            send_sem=send_sem.at[chain, step],
+            recv_sem=recv_sem.at[chain, step],
+            device_id=flip("dp", mask),
+            device_id_type=pl.DeviceIdType.MESH,
+        )
+
+    def back_copy(chain, step, start, size):
+        return pltpu.make_async_remote_copy(
+            src_ref=summed.at[span(start, size)],
+            dst_ref=summed.at[span(start, size)],
+            send_sem=back_send.at[chain, step],
+            recv_sem=back_recv.at[chain, step],
+            device_id=flip("dp", orders[chain][step]),
+            device_id_type=pl.DeviceIdType.MESH,
+        )
+
+    starts = [0, half]
+    size = half // 2
+    copies = [out_copy(chain, 0, starts[chain], size) for chain in range(2)]
+    for copy in copies:
+        copy.start()
+    gain_held[0] = gains[...]
+    gain_step = 0
+    small = gain_copy(0)
+    small.start()
+
+    def advance_gains(small, step):
+        small.wait()
+        gain_held[step + 1] = gain_held[step] + gain_landed[step]
+        if step + 1 < len(hops):
+            small = gain_copy(step + 1)
+            small.start()
+        return small
+
+    for step in range(steps):
+        for chain in range(2):
+            mask = orders[chain][step]
+            bit = (me // mask) % 2
+            copies[chain].wait()
+            mine = span(starts[chain] + bit * size, size)
+            base = chain * half + half - 2 * size
+            source = whole if step == 0 else kept
+            total = source[mine, :] + landed[pl.ds(base, size), :]
+            starts[chain] = starts[chain] + bit * size
+            if step + 1 < steps:
+                kept[mine, :] = total
+                copies[chain] = out_copy(chain, step + 1, starts[chain], size // 2)
+            else:
+                summed[mine, :] = total
+                copies[chain] = back_copy(chain, step, starts[chain], size)
+            copies[chain].start()
+        if step + 1 < steps:
+            size = size // 2
+        if gain_step < len(hops):
+            small = advance_gains(small, gain_step)
+            gain_step += 1
+    for step in reversed(range(steps)):
+        for chain in range(2):
+            copies[chain].wait()
+            bit = (me // orders[chain][step]) % 2
+            starts[chain] = starts[chain] - bit * size
+            if step > 0:
+                copies[chain] = back_copy(chain, step - 1, starts[chain], 2 * size)
+                copies[chain].start()
+        size = size * 2
+        if gain_step < len(hops):
+            small = advance_gains(small, gain_step)
+            gain_step += 1
+    gain_sum[...] = gain_held[len(hops)]
+
+
+def late_sum(whole, gains, dp_size):
+    steps = len(masks_of(dp_size))
+    hops = steps + 2
+    vmem = pl.BlockSpec(memory_space=pltpu.VMEM)
+    return pl.pallas_call(
+        functools.partial(late_kernel, dp_size),
+        out_shape=(
+            jax.ShapeDtypeStruct(whole.shape, jnp.float32),
+            jax.ShapeDtypeStruct(gains.shape, jnp.float32),
+        ),
+        in_specs=[vmem, vmem],
+        out_specs=(vmem, vmem),
+        scratch_shapes=[
+            pltpu.VMEM(whole.shape, jnp.float32),
+            pltpu.VMEM(whole.shape, jnp.float32),
+            pltpu.VMEM((hops + 1,) + gains.shape, jnp.float32),
+            pltpu.VMEM((hops,) + gains.shape, jnp.float32),
+            pltpu.SemaphoreType.DMA((2, steps)),
+            pltpu.SemaphoreType.DMA((2, steps)),
+            pltpu.SemaphoreType.DMA((2, steps)),
+            pltpu.SemaphoreType.DMA((2, steps)),
+            pltpu.SemaphoreType.DMA((hops,)),
+            pltpu.SemaphoreType.DMA((hops,)),
+        ],
+        compiler_params=pltpu.CompilerParams(
+            collective_id=0, has_side_effects=True, vmem_limit_bytes=32 * 1024 * 1024
+        ),
+        cost_estimate=pl.CostEstimate(flops=0, bytes_accessed=100000000, transcendentals=0),
+    )(whole, gains)
 
 
 def per_device(
@@ -198,31 +355,31 @@
         part_other = product(rows_of(rows_in, 1 - core, half_rows))
         arrived = across(part_other, 1)
         part_mine = product(rows_of(rows_in, core, half_rows))
-        mine = part_mine + arrived
-        return mine + across(mine, 2)
-
-    grad_hidden_two = tensor_sum(
+        return part_mine + arrived
+
+    hidden_two_half = tensor_sum(
         lambda rows: jnp.einsum("tcf,cdf->td", rows, up_weight, preferred_element_type=float32),
         grad_up_parts,
     )
+    hidden_two_came = across(hidden_two_half, 2)
+    mlp_half = tensor_sum(
+        lambda rows: jnp.dot(rows, down_weight, preferred_element_type=float32), activated
+    )
+    grad_down = jnp.einsum("tf,td->fd", activated, out_cotangent, preferred_element_type=float32)
+    grad_up = jnp.einsum("td,tcf->cfd", hidden_two, grad_up_parts, preferred_element_type=float32)
+    gain_grad_two = jnp.einsum("cfd,cdf->d", grad_up, up_weight.astype(float32)) / gain_two
+    hidden_two_came, mlp_half, _, _ = lax.optimization_barrier(
+        (hidden_two_came, mlp_half, grad_up, grad_down)
+    )
+    grad_up, grad_down = lax.psum((grad_up, grad_down), "dp")
+    grad_hidden_two = hidden_two_half + hidden_two_came
+    mlp_came = across(mlp_half, 2)
     cot_mine = rows_of(out_cotangent, core, half_rows).astype(float32)
     cot_other = rows_of(out_cotangent, 1 - core, half_rows).astype(float32)
     norm_two_part = norm_two_pull(grad_hidden_two)[0]
     branch_mine = (cot_mine + norm_two_part).astype(bfloat)
     branch_other = (cot_other + across(norm_two_part, 1)).astype(bfloat)
     grad_branch = place_two(branch_mine, branch_other, core).reshape(token_rows, width)
-
-    mlp_branch = tensor_sum(
-        lambda rows: jnp.dot(rows, down_weight, preferred_element_type=float32), activated
-    )
-    both_branches = attn_branch + mlp_branch
-    out_mine = (layer_mine + both_branches).astype(bfloat)
-    out_other = (layer_other + across(both_branches, 1)).astype(bfloat)
-    layer_out = place_two(out_mine, out_other, core).reshape(token_rows, width)
-
-    grad_down = jnp.einsum("tf,td->fd", activated, out_cotangent, preferred_element_type=float32)
-    grad_up = jnp.einsum("td,tcf->cfd", hidden_two, grad_up_parts, preferred_element_type=float32)
-    gain_grad_two = jnp.einsum("cfd,cdf->d", grad_up, up_weight.astype(float32)) / gain_two
 
     grad_out = jnp.einsum("te,td->ed", attended, grad_branch, preferred_element_type=float32)
     grad_attended = jnp.einsum("td,ed->te", grad_branch, out_weight, preferred_element_type=float32)
@@ -253,7 +410,13 @@
     grad_projected = jnp.stack([grad_query_proj, grad_key_proj, grad_value_proj], axis=1).astype(
         bfloat
     )
-    grad_hidden_one = tensor_sum(
+    mlp_came, grad_projected = lax.optimization_barrier((mlp_came, grad_projected))
+    both_branches = attn_branch + (mlp_half + mlp_came)
+    out_mine = (layer_mine + both_branches).astype(bfloat)
+    out_other = (layer_other + across(both_branches, 1)).astype(bfloat)
+    layer_out = place_two(out_mine, out_other, core).reshape(token_rows, width)
+
+    hidden_one_half = tensor_sum(
         lambda rows: jnp.einsum("tce,cde->td", rows, qkv_weight, preferred_element_type=float32),
         grad_projected,
     )
@@ -261,25 +424,24 @@
         "td,tce->ced", hidden_one, grad_projected, preferred_element_type=float32
     )
     gain_grad_one = jnp.einsum("ced,cde->d", grad_qkv, qkv_weight.astype(float32)) / gain_one
-    gains = jnp.stack([gain_grad_one, gain_grad_two])
-    for mask in (1, 2):
-        gains = gains + across(gains, mask)
-    mask = 1
-    while mask < dp_size:
-        gains = gains + swap(gains, "dp", mask, dp_size)
-        mask *= 2
-
+    hidden_one_came = across(hidden_one_half, 2)
+    gains = jnp.stack([gain_grad_one, gain_grad_two] + [jnp.zeros((width,), float32)] * 6)
+    late = [grad_qkv.reshape(3 * columns, width), grad_out]
+    late_rows = 3 * columns + grad_out.shape[0]
+    unit = 16 * dp_size
+    padded = -(-late_rows // unit) * unit
+    if padded > late_rows:
+        late.append(jnp.zeros((padded - late_rows, width), float32))
+    late, gains = late_sum(jnp.concatenate(late, axis=0), gains, dp_size)
+    grad_hidden_one = hidden_one_half + hidden_one_came
     norm_one_pull = jax.vjp(lambda rows: layer_norm(rows, gain_one), layer_mine)[1]
     both_norms = norm_two_part + norm_one_pull(grad_hidden_one)[0]
     input_mine = (cot_mine + both_norms).astype(bfloat)
     input_other = (cot_other + across(both_norms, 1)).astype(bfloat)
     input_grad = place_two(input_mine, input_other, core).reshape(token_rows, width)
 
-    grad_up, grad_down = lax.psum((grad_up, grad_down), "dp")
-    grad_qkv, grad_out, grad_up, grad_down = lax.optimization_barrier(
-        (grad_qkv, grad_out, grad_up, grad_down)
-    )
-    grad_qkv, grad_out = lax.psum((grad_qkv, grad_out), "dp")
+    grad_qkv = late[: 3 * columns].reshape(3, columns, width)
+    grad_out = late[3 * columns : late_rows]
     grad_up = grad_up.transpose(0, 2, 1)
     grad_qkv = grad_qkv.transpose(0, 2, 1)
     return (layer_out, input_grad, grad_qkv, grad_out, grad_up, grad_down, gains[0], gains[1])

time: 414 us -> 354 us (0.86)
  waiting for transfers between devices: 262 us -> 108 us
  Pallas kernels: 0 us -> 109 us
  other arithmetic: 47.5 us -> 41.6 us
  matrix products: 38.7 us -> 33 us
  starting transfers between devices: 16.3 us -> 10.9 us
    pallas_call x0 -> x1, Pallas kernels: none -> 109 us  [late_sum(): pl.pallas_call(functools.partial(late_kernel, dp_size), out_shape=(jax.Sh...]
    psum x1 -> x0, waiting for transfers between devices: 81.7 us -> none  [per_device(): grad_qkv, grad_out = lax.psum((grad_qkv, grad_out), 'dp')]
    psum x1, waiting for transfers between devices: 73.6 us -> 0.01 us  [per_device(): grad_up, grad_down = lax.psum((grad_up, grad_down), 'dp')]
    ppermute x21 -> x16, starting transfers between devices: 16.3 us -> 10.9 us  [swap(): return lax.ppermute(array, axis, [(i, i ^ mask) for i in range(size)])]
    unnamed x149 -> x109, local copies, waits for them, and re-layouts: 20.6 us -> 17.9 us
    ppermute x21 -> x16, waiting for transfers between devices: 106 us -> 108 us  [swap(): return lax.ppermute(array, axis, [(i, i ^ mask) for i in range(size)])]
  transfers between devices with their start and end apart: 23 -> 17, of which waited for: 13 -> 8; matrix products, arithmetic and copies ran while one was open for 15% -> 15% of each run, Pallas kernels for 0% -> 31%
where the time goes in v3:
time: 354 us; the launch traced here: 353 us
  Pallas kernels  109 us (31%)
  waiting for transfers between devices  108 us (31%)
  other arithmetic  41.6 us (12%)
  local copies, waits for them, and re-layouts  34.6 us (10%)
  matrix products  33 us (9%)
  between operations  15.8 us (4%)
  starting transfers between devices  10.9 us (3%)
    pallas_call x1, Pallas kernels, late_sum(): pl.pallas_call(functools.partial(late_kernel, dp_size), out_shape=(jax.Sh...  109 us
    ppermute x16, waiting for transfers between devices, swap(): return lax.ppermute(array, axis, [(i, i ^ mask) for i in range(size)])  108 us
    unnamed x109, local copies, waits for them, and re-layouts  17.9 us
    ppermute x16, starting transfers between devices, swap(): return lax.ppermute(array, axis, [(i, i ^ mask) for i in range(size)])  10.9 us
  transfers between devices with their start and end apart: 17, of which 8 were waited for; matrix products, arithmetic and copies ran while one was open for 15% of the time, Pallas kernels for 31%

profile of v3, /device:TPU:0, one launch (start us, length us, event | category | flops | bytes accessed | tf_op | source)
XLA Modules:
  0.0 353.0 jit_solution(3195076525097113130)
XLA Ops:
  7.2 1.3 slice.140
  11.5 1.8 convert_reduce_fusion
  14.0 1.3 fusion.126
  15.3 1.6 slice_bitcast_fusion.3
  18.6 1.0 copy-done.19
  19.8 1.1 fusion.99
  21.8 1.9 fusion.97
  27.0 0.9 fusion.18
  28.4 1.1 fusion.135
  29.5 1.2 fusion
  31.8 2.4 multiply_bitcast_fusion.1
  34.9 0.9 constant_dynamic-slice_fusion
  36.2 2.6 collective-permute-start.2
  40.1 1.6 collective-permute-start.1
  41.8 1.0 bitcast_dynamic-update-slice_fusion.2
  42.9 1.9 convert_element_type.132
  44.7 1.3 copy.31
  46.2 1.0 fusion.103
  47.3 22.7 %collective-permute-done.1 = f32[512,192]{0,1:T(8,128)} collective-permute-done((f32[512,192]{0,1:T(8,128)}, f32[512,192]{0,1:T(8,128)}, u32[]{:S(2)}, u32[]{:S(2)}) %collective-permute-start.1) | collective-permute-done | bytes 393248 | tf_op jit(solution)/shard_map/ppermute | solution.py:65
  69.9 1.0 fusion.105
  71.1 1.2 fusion.107
  72.3 1.1 fusion.88
  73.4 1.1 fusion.90
  74.6 2.0 fusion.130
  76.9 1.3 broadcast.277.clone.1
  78.2 1.7 fusion.42
  80.5 2.1 fusion.136
  82.5 1.3 collective-permute-done.6
  83.8 2.4 fusion.44
  86.2 2.5 convolution_bitcast_fusion
  88.8 2.8 multiply_convert_fusion.4
  94.3 2.2 collective-permute-done.7
  97.4 1.5 collective-permute-start.8
  98.8 1.5 fusion.137
  100.4 3.7 %multiply_reduce_fusion.2 = (f32[768]{0:T(1024)S(1)}, f32[2,288,768]{2,1,0:T(8,128)}) fusion(bf16[2,768,288]{1,2,0:T(8,128)(2,1)S(1)} %copy-done.38, bf16[1024,768,1]{1,0,2:T(8,128)(2,1)} %bitcast.32, bf16[1024,1,288]{0,2,1:T(8,128)(2,1)S(1)} %get-tuple-element.42, bf16[1024,1,288]{0,2,1:T(8,128)(2,1)S(1)} %get-tuple-element.43), kind=kOutput, calls=%fused_computation.22 | convolution fusion | flops 907885824 | bytes 5409792 | tf_op jit(solution)/shard_map/td,tcf->cfd/dot_general | solution.py:369
  104.1 1.8 convolution_add_fusion
  105.9 28.3 %collective-permute-done.8 = f32[512,768]{1,0:T(8,128)S(1)} collective-permute-done((f32[512,768]{1,0:T(8,128)S(1)}, f32[512,768]{1,0:T(8,128)S(1)}, u32[]{:S(2)}, u32[]{:S(2)}) %collective-permute-start.8) | collective-permute-done | bytes 1572896 | tf_op jit(solution)/shard_map/ppermute | solution.py:65
  135.9 1.4 collective-permute-start.10
  137.3 2.0 collective-permute-done.11
  139.5 1.2 copy-done.10
  141.4 1.8 multiply_reduce_fusion
  143.3 1.2 fusion.6
  144.5 1.4 multiply_convert_fusion
  146.5 1.0 fusion.131
  147.9 1.0 copy.36
  148.9 2.0 stack_reshape_reshape.4
  150.9 3.3 fusion.19
  155.7 17.3 %collective-permute-done.10 = f32[512,768]{1,0:T(8,128)} collective-permute-done((f32[512,768]{1,0:T(8,128)}, f32[512,768]{1,0:T(8,128)}, u32[]{:S(2)}, u32[]{:S(2)}) %collective-permute-start.10) | collective-permute-done | bytes 1572896 | tf_op jit(solution)/shard_map/ppermute | solution.py:65
  174.0 3.4 collective-permute-done.13
  177.4 2.0 bitcast_add_fusion
  179.4 1.3 collective-permute-start.14
  181.0 1.8 copy-done.4
  182.8 2.8 fusion.46
  185.6 30.5 %collective-permute-done.14 = f32[512,768]{1,0:T(8,128)} collective-permute-done((f32[512,768]{1,0:T(8,128)}, f32[512,768]{1,0:T(8,128)}, u32[]{:S(2)}, u32[]{:S(2)}) %collective-permute-start.14) | collective-permute-done | bytes 1572896 | tf_op jit(solution)/shard_map/ppermute | solution.py:65
  216.1 2.4 multiply_reduce_fusion.5
  218.6 2.7 fusion.127
  221.3 1.2 broadcast.277.clone.3
  223.3 1.2 fusion.54
  225.6 1.3 multiply_reduce_fusion.3
  227.8 109.4 %shard_map.152 = (f32[768,768]{1,0:T(8,128)S(1)}, f32[8,768]{1,0:T(8,128)S(1)}) custom-call(f32[768,768]{1,0:T(8,128)S(1)} %pad_maximum_fusion.whole, f32[8,768]{1,0:T(8,128)S(1)} %maximum_maximum_fusion.gains), custom_call_target="tpu_custom_call" | custom-call | bytes 100000000 | tf_op jit(solution)/shard_map/pallas_call | solution.py:210
  337.2 1.3 slice.161
  340.2 1.1 copy-done.28
  341.3 1.0 fusion.50
  342.3 2.9 copy.110
  (205 shorter events, 29.0 us)
Async XLA Ops:
  7.2 73.3 %copy-start = (bf16[288,768]{1,0:T(8,128)(2,1)S(1)}, bf16[288,768]{1,0:T(8,128)(2,1)}, u32[]{:S(2)}) copy-start(bf16[288,768]{1,0:T(8,128)(2,1)} %param.14) | copy-start | bytes 1327108
  7.2 6.1 %copy-start.5 = (bf16[1024,768]{1,0:T(8,128)(2,1)S(1)}, bf16[1024,768]{1,0:T(8,128)(2,1)}, u32[]{:S(2)}) copy-start(bf16[1024,768]{1,0:T(8,128)(2,1)} %param.9) | copy-start | bytes 4718596
  7.2 335.1 %all-reduce.14.cloned.1.call-start = ((), (), s32[]{:S(2)}) async-start(), calls=%async_computation | async-start | bytes 5308416 | tf_op jit(solution)/shard_map/psum | solution.py:374
  11.5 2.4 copy-start.44
  11.5 2.4 copy-start.34
  18.5 1.1 copy-start.19
  21.0 0.7 copy-start.22
  21.7 2.3 copy-start.18
  24.0 1.1 copy-start.17
  24.1 1.2 copy-start.31
  25.1 1.0 copy-start.29
  26.2 0.7 copy-start.42
  26.5 1.8 copy-start.40
  26.5 1.8 copy-start.41
  28.2 1.3 copy-start.39
  28.3 1.2 copy-start.26
  29.5 2.3 copy-start.2
  31.8 2.4 copy-start.24
  34.7 4.2 %copy-start.32 = (bf16[192,768]{1,0:T(8,128)(2,1)S(1)}, bf16[192,768]{1,0:T(8,128)(2,1)}, u32[]{:S(2)}) copy-start(bf16[192,768]{1,0:T(8,128)(2,1)} %param.12) | copy-start | bytes 884740
  35.8 10.4 %collective-permute-start = (f32[512,192]{0,1:T(8,128)}, f32[512,192]{0,1:T(8,128)}, u32[]{:S(2)}, u32[]{:S(2)}) collective-permute-start(f32[512,192]{0,1:T(8,128)} %get-tuple-element.58), channel_id=1, source_target_pairs={{0,1},{1,0},{2,3},{3,2},{4,5},{5,4},{6,7},{7,6},{8,9},{9,8},{10,11... | collective-permute-start | bytes 1179656 | tf_op jit(solution)/shard_map/ppermute | solution.py:65
  36.2 34.8 %collective-permute-start.2 = (f32[512,192]{0,1:T(8,128)}, f32[512,192]{0,1:T(8,128)}, u32[]{:S(2)}, u32[]{:S(2)}) collective-permute-start(f32[512,192]{0,1:T(8,128)} %get-tuple-element.58), channel_id=1, source_target_pairs={{0,3},{1,2},{2,1},{3,0},{4,7},{5,6},{6,5},{7,4},{8,11},{9,10},{10,... | collective-permute-start | bytes 1179656 | tf_op jit(solution)/shard_map/ppermute | solution.py:65
  39.7 32.5 %collective-permute-start.3 = (f32[192,768]{1,0:T(8,128)}, f32[192,768]{1,0:T(8,128)}, u32[]{:S(2)}, u32[]{:S(2)}) collective-permute-start(f32[192,768]{1,0:T(8,128)} %convert_multiply_fusion), channel_id=1, source_target_pairs={{0,1},{1,0},{2,3},{3,2},{4,5},{5,4},{6,7},{7,6},{8,9},{9,8},{10,11... | collective-permute-start | bytes 1769480 | tf_op jit(solution)/shard_map/ppermute | solution.py:65
  39.7 31.2 %collective-permute-start.4 = (f32[192,768]{1,0:T(8,128)}, f32[192,768]{1,0:T(8,128)}, u32[]{:S(2)}, u32[]{:S(2)}) collective-permute-start(f32[192,768]{1,0:T(8,128)} %convert_multiply_fusion), channel_id=1, source_target_pairs={{0,2},{1,3},{2,0},{3,1},{4,6},{5,7},{6,4},{7,5},{8,10},{9,11},{10,... | collective-permute-start | bytes 1769480 | tf_op jit(solution)/shard_map/ppermute | solution.py:65
  40.1 29.8 %collective-permute-start.1 = (f32[512,192]{0,1:T(8,128)}, f32[512,192]{0,1:T(8,128)}, u32[]{:S(2)}, u32[]{:S(2)}) collective-permute-start(f32[512,192]{0,1:T(8,128)} %get-tuple-element.57), channel_id=1, source_target_pairs={{0,2},{1,3},{2,0},{3,1},{4,6},{5,7},{6,4},{7,5},{8,10},{9,11},{10,... | collective-permute-start | bytes 1179656 | tf_op jit(solution)/shard_map/ppermute | solution.py:65
  44.7 1.4 copy-start.43
  46.0 25.0 %copy-start.15 = (bf16[8,128,3,64]{1,0,3,2:T(8,128)(2,1)}, bf16[8,128,3,64]{1,0,3,2:T(8,128)(2,1)S(1)}, u32[]{:S(2)}) copy-start(bf16[8,128,3,64]{1,0,3,2:T(8,128)(2,1)S(1)} %copy.31) | copy-start | bytes 1179652
  71.0 3.6 %copy-start.3 = (f32[1024,768]{1,0:T(8,128)S(1)}, f32[1024,768]{1,0:T(8,128)}, u32[]{:S(2)}) copy-start(f32[1024,768]{1,0:T(8,128)} %convert_element_type.132) | copy-start | bytes 9437188
  71.0 3.5 collective-permute-start.5
  79.8 4.0 %collective-permute-start.6 = (f32[512,768]{1,0:T(8,128)}, f32[512,768]{1,0:T(8,128)}, u32[]{:S(2)}, u32[]{:S(2)}) collective-permute-start(f32[512,768]{1,0:T(8,128)} %get-tuple-element.39), channel_id=1, source_target_pairs={{0,1},{1,0},{2,3},{3,2},{4,5},{5,4},{6,7},{7,6},{8,9},{9,8},{10,11... | collective-permute-start | bytes 4718600 | tf_op jit(solution)/shard_map/ppermute | solution.py:65
  82.5 3.7 %copy-start.38 = (bf16[2,768,288]{1,2,0:T(8,128)(2,1)S(1)}, bf16[2,768,288]{1,2,0:T(8,128)(2,1)}, u32[]{:S(2)}) copy-start(bf16[2,768,288]{1,2,0:T(8,128)(2,1)} %param.13) | copy-start | bytes 2654212
  93.1 3.5 collective-permute-start.7
  94.1 4.7 %copy-start.7 = (bf16[1024,768]{1,0:T(8,128)(2,1)S(1)}, bf16[1024,768]{1,0:T(8,128)(2,1)}, u32[]{:S(2)}) copy-start(bf16[1024,768]{1,0:T(8,128)(2,1)} %param.17) | copy-start | bytes 4718596
  94.1 10.0 %collective-permute-start.9 = (f32[512,768]{1,0:T(8,128)S(1)}, f32[512,768]{1,0:T(8,128)S(1)}, u32[]{:S(2)}, u32[]{:S(2)}) collective-permute-start(f32[512,768]{1,0:T(8,128)S(1)} %fusion.93), channel_id=1, source_target_pairs={{0,1},{1,0},{2,3},{3,2},{4,5},{5,4},{6,7},{7,6},{8,9},{9,8},{10,11... | collective-permute-start | bytes 4718600 | tf_op jit(solution)/shard_map/ppermute | solution.py:65
  97.4 36.7 %collective-permute-start.8 = (f32[512,768]{1,0:T(8,128)S(1)}, f32[512,768]{1,0:T(8,128)S(1)}, u32[]{:S(2)}, u32[]{:S(2)}) collective-permute-start(f32[512,768]{1,0:T(8,128)S(1)} %bitcast_add_fusion.1), channel_id=1, source_target_pairs={{0,2},{1,3},{2,0},{3,1},{4,6},{5,7},{6,4},{7,5},{8,10},{9,11},{10,... | collective-permute-start | bytes 4718600 | tf_op jit(solution)/shard_map/ppermute | solution.py:65
  135.4 6.0 %slice-start = ((s8[4718592]{0:T(1024)(128)(4,1)}), s8[4194304]{0:T(1024)(128)(4,1)S(1)}, s32[]{:S(2)}) async-start(s8[4718592]{0:T(1024)(128)(4,1)} %bitcast.358), calls=%async_computation.1 | async-start | bytes 8388608
  135.5 5.9 %slice-start.1 = ((s8[4718592]{0:T(1024)(128)(4,1)}), s8[524288]{0:T(1024)(128)(4,1)S(1)}, s32[]{:S(2)}) async-start(s8[4718592]{0:T(1024)(128)(4,1)} %bitcast.358), calls=%async_computation.2 | async-start | bytes 1048576
  135.8 3.7 %copy-start.12 = (f32[512,768]{1,0:T(8,128)}, f32[512,768]{1,0:T(8,128)S(1)}, u32[]{:S(2)}) copy-start(f32[512,768]{1,0:T(8,128)S(1)} %get-tuple-element.33) | copy-start | bytes 4718596
  135.8 3.5 collective-permute-start.11
  135.9 37.2 %collective-permute-start.10 = (f32[512,768]{1,0:T(8,128)}, f32[512,768]{1,0:T(8,128)}, u32[]{:S(2)}, u32[]{:S(2)}) collective-permute-start(f32[512,768]{1,0:T(8,128)} %convolution_add_fusion), channel_id=1, source_target_pairs={{0,2},{1,3},{2,0},{3,1},{4,6},{5,7},{6,4},{7,5},{8,10},{9,11},{10,... | collective-permute-start | bytes 4718600 | tf_op jit(solution)/shard_map/ppermute | solution.py:65
  139.2 1.5 copy-start.33
  139.5 1.2 copy-start.10
  139.5 1.9 copy-start.25
  144.5 1.4 copy-start.27
  145.9 1.8 copy-start.9
  150.9 3.3 copy-start.14
  150.9 3.3 copy-start.23
  154.6 1.0 copy-start.30
  154.9 18.1 %copy-start.35 = (bf16[3,768,192]{1,2,0:T(8,128)(2,1)S(1)}, bf16[3,768,192]{1,2,0:T(8,128)(2,1)}, u32[]{:S(2)}) copy-start(bf16[3,768,192]{1,2,0:T(8,128)(2,1)} %param.11) | copy-start | bytes 2654212
  155.7 21.7 %copy-start.20 = (bf16[1024,3,192]{0,2,1:T(8,128)(2,1)}, bf16[1024,3,192]{0,2,1:T(8,128)(2,1)S(1)}, u32[]{:S(2)}) copy-start(bf16[1024,3,192]{0,2,1:T(8,128)(2,1)S(1)} %pad_maximum_fusion.4) | copy-start | bytes 3538948
  173.9 3.5 collective-permute-start.13
  179.4 36.8 %collective-permute-start.14 = (f32[512,768]{1,0:T(8,128)}, f32[512,768]{1,0:T(8,128)}, u32[]{:S(2)}, u32[]{:S(2)}) collective-permute-start(f32[512,768]{1,0:T(8,128)} %bitcast_add_fusion), channel_id=1, source_target_pairs={{0,2},{1,3},{2,0},{3,1},{4,6},{5,7},{6,4},{7,5},{8,10},{9,11},{10,... | collective-permute-start | bytes 4718600 | tf_op jit(solution)/shard_map/ppermute | solution.py:65
  180.9 1.9 copy-start.4
  185.6 154.4 %collective-permute-start.12 = (f32[512,768]{1,0:T(8,128)S(1)}, f32[512,768]{1,0:T(8,128)S(1)}, u32[]{:S(2)}, u32[]{:S(2)}) collective-permute-start(f32[512,768]{1,0:T(8,128)S(1)} %get-tuple-element.31), channel_id=1, source_target_pairs={{0,1},{1,0},{2,3},{3,2},{4,5},{5,4},{6,7},{7,6},{8,9},{9,8},{10,11... | collective-permute-start | bytes 4718600 | tf_op jit(solution)/shard_map/ppermute | solution.py:65
  218.6 4.0 %copy-start.13 = (f32[512,768]{1,0:T(8,128)S(1)}, f32[512,768]{1,0:T(8,128)}, u32[]{:S(2)}) copy-start(f32[512,768]{1,0:T(8,128)} %copy-done.12) | copy-start | bytes 4718596
  221.3 2.0 copy-start.8
  223.3 1.8 copy-start.6
  223.3 2.1 copy-start.21
  223.3 2.4 copy-start.36
  224.5 2.5 copy-start.11
  224.5 2.5 copy-start.16
  224.5 115.6 %collective-permute-start.15 = (f32[512,768]{1,0:T(8,128)S(1)}, f32[512,768]{1,0:T(8,128)S(1)}, u32[]{:S(2)}, u32[]{:S(2)}) collective-permute-start(f32[512,768]{1,0:T(8,128)S(1)} %get-tuple-element.27), channel_id=1, source_target_pairs={{0,1},{1,0},{2,3},{3,2},{4,5},{5,4},{6,7},{7,6},{8,9},{9,8},{10,11... | collective-permute-start | bytes 4718600 | tf_op jit(solution)/shard_map/ppermute | solution.py:65
  340.1 1.1 copy-start.28
  342.3 2.9 copy-start.37
  342.3 3.8 %copy-start.1 = (bf16[288,768]{1,0:T(8,128)(2,1)S(1)}, bf16[288,768]{1,0:T(8,128)(2,1)}, u32[]{:S(2)}) copy-start(bf16[288,768]{1,0:T(8,128)(2,1)} %param.14) | copy-start | bytes 1327108
Sparse Core Ops, SparseCore 0:
  181.0 150.9 all-reduce.13

commit v4 on v3

--- a/solution.py
+++ b/solution.py
@@ -88,15 +88,29 @@
     return masks
 
 
-def late_kernel(dp_size, whole, gains, summed, gain_sum, kept, landed, gain_held, gain_landed, *sems):
+def chains_of(rows, dp_size):
+    unit = 8 * dp_size
+    units = rows // unit
+    count = min(4, units)
+    masks = masks_of(dp_size)
+    chains = []
+    start = 0
+    for index in range(count):
+        size = (units // count + (1 if index >= count - units % count else 0)) * unit
+        order = masks[1:] + masks[:1] if index == 1 else masks
+        chains.append((start, size, order))
+        start += size
+    return chains
+
+
+def sum_kernel(dp_size, whole, gains, summed, gain_sum, kept, landed, gain_held, gain_landed, *sems):
     send_sem, recv_sem, back_send, back_recv, gain_send, gain_recv = sems
     me = lax.axis_index("dp")
     lane = lax.axis_index("tensor")
     masks = masks_of(dp_size)
     steps = len(masks)
-    rows = whole.shape[0]
-    half = rows // 2
-    orders = (masks, masks[1:] + masks[:1])
+    chains = chains_of(whole.shape[0], dp_size)
+    orders = [order for _, _, order in chains]
     hops = [("tensor", 1), ("tensor", 2)] + [("dp", mask) for mask in masks]
 
     def flip(axis, mask):
@@ -127,7 +141,7 @@
     def out_copy(chain, step, start, size):
         mask = orders[chain][step]
         bit = (me // mask) % 2
-        base = chain * half + half - 2 * size
+        base = chains[chain][0] + chains[chain][1] - 2 * size
         source = whole if step == 0 else kept
         return pltpu.make_async_remote_copy(
             src_ref=source.at[span(start + (1 - bit) * size, size)],
@@ -148,9 +162,9 @@
             device_id_type=pl.DeviceIdType.MESH,
         )
 
-    starts = [0, half]
-    size = half // 2
-    copies = [out_copy(chain, 0, starts[chain], size) for chain in range(2)]
+    starts = [start for start, _, _ in chains]
+    sizes = [size // 2 for _, size, _ in chains]
+    copies = [out_copy(chain, 0, starts[chain], sizes[chain]) for chain in range(len(chains))]
     for copy in copies:
         copy.start()
     gain_held[0] = gains[...]
@@ -167,12 +181,13 @@
         return small
 
     for step in range(steps):
-        for chain in range(2):
+        for chain in range(len(chains)):
+            size = sizes[chain]
             mask = orders[chain][step]
             bit = (me // mask) % 2
             copies[chain].wait()
             mine = span(starts[chain] + bit * size, size)
-            base = chain * half + half - 2 * size
+            base = chains[chain][0] + chains[chain][1] - 2 * size
             source = whole if step == 0 else kept
             total = source[mine, :] + landed[pl.ds(base, size), :]
             starts[chain] = starts[chain] + bit * size
@@ -183,32 +198,42 @@
                 summed[mine, :] = total
                 copies[chain] = back_copy(chain, step, starts[chain], size)
             copies[chain].start()
-        if step + 1 < steps:
-            size = size // 2
+            if step + 1 < steps:
+                sizes[chain] = size // 2
         if gain_step < len(hops):
             small = advance_gains(small, gain_step)
             gain_step += 1
     for step in reversed(range(steps)):
-        for chain in range(2):
+        for chain in range(len(chains)):
+            size = sizes[chain]
             copies[chain].wait()
             bit = (me // orders[chain][step]) % 2
             starts[chain] = starts[chain] - bit * size
             if step > 0:
                 copies[chain] = back_copy(chain, step - 1, starts[chain], 2 * size)
                 copies[chain].start()
-        size = size * 2
+            sizes[chain] = size * 2
         if gain_step < len(hops):
             small = advance_gains(small, gain_step)
             gain_step += 1
     gain_sum[...] = gain_held[len(hops)]
 
 
-def late_sum(whole, gains, dp_size):
+def dp_sum(pieces, gain, dp_size, collective_id):
+    width = gain.shape[0]
+    rows = sum(piece.shape[0] for piece in pieces)
+    unit = 8 * dp_size
+    padded = -(-rows // unit) * unit
+    if padded > rows:
+        pieces = pieces + [jnp.zeros((padded - rows, width), jnp.float32)]
+    whole = jnp.concatenate(pieces, axis=0)
+    gains = jnp.concatenate([gain[None], jnp.zeros((7, width), jnp.float32)], axis=0)
     steps = len(masks_of(dp_size))
+    count = len(chains_of(padded, dp_size))
     hops = steps + 2
     vmem = pl.BlockSpec(memory_space=pltpu.VMEM)
-    return pl.pallas_call(
-        functools.partial(late_kernel, dp_size),
+    summed, gains = pl.pallas_call(
+        functools.partial(sum_kernel, dp_size),
         out_shape=(
             jax.ShapeDtypeStruct(whole.shape, jnp.float32),
             jax.ShapeDtypeStruct(gains.shape, jnp.float32),
@@ -220,18 +245,15 @@
             pltpu.VMEM(whole.shape, jnp.float32),
             pltpu.VMEM((hops + 1,) + gains.shape, jnp.float32),
             pltpu.VMEM((hops,) + gains.shape, jnp.float32),
-            pltpu.SemaphoreType.DMA((2, steps)),
-            pltpu.SemaphoreType.DMA((2, steps)),
-            pltpu.SemaphoreType.DMA((2, steps)),
-            pltpu.SemaphoreType.DMA((2, steps)),
-            pltpu.SemaphoreType.DMA((hops,)),
-            pltpu.SemaphoreType.DMA((hops,)),
-        ],
+        ]
+        + [pltpu.SemaphoreType.DMA((count, steps))] * 4
+        + [pltpu.SemaphoreType.DMA((hops,))] * 2,
         compiler_params=pltpu.CompilerParams(
-            collective_id=0, has_side_effects=True, vmem_limit_bytes=32 * 1024 * 1024
+            collective_id=collective_id, has_side_effects=True, vmem_limit_bytes=32 * 1024 * 1024
         ),
-        cost_estimate=pl.CostEstimate(flops=0, bytes_accessed=100000000, transcendentals=0),
+        cost_estimate=pl.CostEstimate(flops=0, bytes_accessed=200000000, transcendentals=0),
     )(whole, gains)
+    return summed[:rows], gains[0]
 
 
 def per_device(
@@ -362,18 +384,25 @@
         grad_up_parts,
     )
     hidden_two_came = across(hidden_two_half, 2)
+    activated_after, _ = lax.optimization_barrier((activated, hidden_two_half))
     mlp_half = tensor_sum(
-        lambda rows: jnp.dot(rows, down_weight, preferred_element_type=float32), activated
-    )
+        lambda rows: jnp.dot(rows, down_weight, preferred_element_type=float32), activated_after
+    )
+    mlp_came = across(mlp_half, 2)
     grad_down = jnp.einsum("tf,td->fd", activated, out_cotangent, preferred_element_type=float32)
     grad_up = jnp.einsum("td,tcf->cfd", hidden_two, grad_up_parts, preferred_element_type=float32)
+    units = grad_down.shape[0]
     gain_grad_two = jnp.einsum("cfd,cdf->d", grad_up, up_weight.astype(float32)) / gain_two
-    hidden_two_came, mlp_half, _, _ = lax.optimization_barrier(
-        (hidden_two_came, mlp_half, grad_up, grad_down)
-    )
-    grad_up, grad_down = lax.psum((grad_up, grad_down), "dp")
+    grad_up, grad_down, gain_grad_two, mlp_half = lax.optimization_barrier(
+        (grad_up, grad_down, gain_grad_two, mlp_half)
+    )
+    early, gain_grad_two = dp_sum(
+        [grad_up.reshape(2 * units, width), grad_down], gain_grad_two, dp_size, 1
+    )
+    hidden_two_came, mlp_came, early = lax.optimization_barrier((hidden_two_came, mlp_came, early))
+    grad_up = early[: 2 * units].reshape(2, units, width).transpose(0, 2, 1)
+    grad_down = early[2 * units :]
     grad_hidden_two = hidden_two_half + hidden_two_came
-    mlp_came = across(mlp_half, 2)
     cot_mine = rows_of(out_cotangent, core, half_rows).astype(float32)
     cot_other = rows_of(out_cotangent, 1 - core, half_rows).astype(float32)
     norm_two_part = norm_two_pull(grad_hidden_two)[0]
@@ -410,7 +439,6 @@
     grad_projected = jnp.stack([grad_query_proj, grad_key_proj, grad_value_proj], axis=1).astype(
         bfloat
     )
-    mlp_came, grad_projected = lax.optimization_barrier((mlp_came, grad_projected))
     both_branches = attn_branch + (mlp_half + mlp_came)
     out_mine = (layer_mine + both_branches).astype(bfloat)
     out_other = (layer_other + across(both_branches, 1)).astype(bfloat)
@@ -425,14 +453,10 @@
     )
     gain_grad_one = jnp.einsum("ced,cde->d", grad_qkv, qkv_weight.astype(float32)) / gain_one
     hidden_one_came = across(hidden_one_half, 2)
-    gains = jnp.stack([gain_grad_one, gain_grad_two] + [jnp.zeros((width,), float32)] * 6)
-    late = [grad_qkv.reshape(3 * columns, width), grad_out]
-    late_rows = 3 * columns + grad_out.shape[0]
-    unit = 16 * dp_size
-    padded = -(-late_rows // unit) * unit
-    if padded > late_rows:
-        late.append(jnp.zeros((padded - late_rows, width), float32))
-    late, gains = late_sum(jnp.concatenate(late, axis=0), gains, dp_size)
+    late, gain_grad_one = dp_sum(
+        [grad_qkv.reshape(3 * columns, width), grad_out], gain_grad_one, dp_size, 0
+    )
+    hidden_one_came, late = lax.optimization_barrier((hidden_one_came, late))
     grad_hidden_one = hidden_one_half + hidden_one_came
     norm_one_pull = jax.vjp(lambda rows: layer_norm(rows, gain_one), layer_mine)[1]
     both_norms = norm_two_part + norm_one_pull(grad_hidden_one)[0]
@@ -441,10 +465,9 @@
     input_grad = place_two(input_mine, input_other, core).reshape(token_rows, width)
 
     grad_qkv = late[: 3 * columns].reshape(3, columns, width)
-    grad_out = late[3 * columns : late_rows]
-    grad_up = grad_up.transpose(0, 2, 1)
+    grad_out = late[3 * columns :]
     grad_qkv = grad_qkv.transpose(0, 2, 1)
-    return (layer_out, input_grad, grad_qkv, grad_out, grad_up, grad_down, gains[0], gains[1])
+    return (layer_out, input_grad, grad_qkv, grad_out, grad_up, grad_down, gain_grad_one, gain_grad_two)
 
 
 def solution(mesh):

time: 354 us -> 325 us (0.918)
  waiting for transfers between devices: 108 us -> 35.5 us
  Pallas kernels: 109 us -> 177 us
  between operations: 15.8 us -> 2.64 us
  matrix products: 33 us -> 26.8 us
  other arithmetic: 41.6 us -> 37 us
    ppermute x16, waiting for transfers between devices: 108 us -> 35.5 us  [swap(): return lax.ppermute(array, axis, [(i, i ^ mask) for i in range(size)])]
    pallas_call x1 -> x2, Pallas kernels: 109 us -> 177 us  [dp_sum(): pl.pallas_call(functools.partial(sum_kernel, dp_size), out_shape=(jax.Sha...]
    slice x3 -> x7, local copies, waits for them, and re-layouts: 1.54 us -> 6.18 us  [the longest x3 2.96 us: dp_sum(): return (summed[:rows], gains[0])]
    unnamed x109 -> x119, local copies, waits for them, and re-layouts: 17.9 us -> 15.6 us
  transfers between devices with their start and end apart: 17 -> 16, of which waited for: 8 -> 6; matrix products, arithmetic and copies ran while one was open for 15% -> 9% of each run, Pallas kernels for 31% -> 55%
where the time goes in v4:
time: 325 us
  Pallas kernels  177 us (54%)
  other arithmetic  37 us (11%)
  waiting for transfers between devices  35.5 us (11%)
  local copies, waits for them, and re-layouts  34.1 us (10%)
  matrix products  26.8 us (8%)
  starting transfers between devices  11.6 us (4%)
    pallas_call x2, Pallas kernels, dp_sum(): pl.pallas_call(functools.partial(sum_kernel, dp_size), out_shape=(jax.Sha...  177 us
    ppermute x16, waiting for transfers between devices, swap(): return lax.ppermute(array, axis, [(i, i ^ mask) for i in range(size)])  35.5 us
    unnamed x119, local copies, waits for them, and re-layouts  15.6 us
    ppermute x16, starting transfers between devices, swap(): return lax.ppermute(array, axis, [(i, i ^ mask) for i in range(size)])  11.6 us
  transfers between devices with their start and end apart: 16, of which 6 were waited for; matrix products, arithmetic and copies ran while one was open for 9% of the time, Pallas kernels for 55%

profile of v4, /device:TPU:0, one launch (start us, length us, event | category | flops | bytes accessed | tf_op | source)
XLA Modules:
  0.0 324.6 jit_solution(902214483049883642)
XLA Ops:
  0.7 1.3 slice.149
  2.7 0.9 select_bitcast_fusion
  5.0 1.8 convert_reduce_fusion
  7.4 1.3 fusion.126
  8.7 1.6 slice_bitcast_fusion.3
  11.4 0.9 copy-done.22
  12.5 1.1 fusion.99
  14.6 1.9 fusion.97
  17.1 0.9 copy-done.20
  19.2 1.0 fusion.18
  20.6 1.1 fusion.135
  21.8 1.2 fusion
  23.9 2.4 multiply_bitcast_fusion.1
  27.0 0.9 constant_dynamic-slice_fusion
  28.4 2.6 collective-permute-start.2
  31.0 0.9 convert_multiply_fusion
  32.3 1.6 collective-permute-start.1
  34.0 1.9 convert_element_type.132
  35.9 1.3 copy.31
  38.2 1.0 fusion.103
  39.2 22.8 %collective-permute-done.1 = f32[512,192]{0,1:T(8,128)} collective-permute-done((f32[512,192]{0,1:T(8,128)}, f32[512,192]{0,1:T(8,128)}, u32[]{:S(2)}, u32[]{:S(2)}) %collective-permute-start.1) | collective-permute-done | bytes 393248 | tf_op jit(solution)/shard_map/ppermute | solution.py:65
  62.1 1.0 fusion.105
  63.2 1.2 fusion.107
  64.4 1.1 fusion.88
  65.5 1.1 fusion.90
  66.7 2.0 fusion.130
  69.0 1.3 broadcast.282.clone.1
  70.3 1.7 fusion.42
  72.6 2.1 fusion.136
  74.7 1.3 collective-permute-done.6
  76.0 2.4 fusion.44
  78.4 2.5 convolution_bitcast_fusion
  80.9 2.8 multiply_convert_fusion.4
  84.4 0.8 convolution_bitcast_fusion.2
  85.6 3.0 collective-permute-done.7
  88.7 0.8 bitcast_add_fusion.1
  90.6 1.4 collective-permute-start.9
  91.9 1.7 collective-permute-done.8
  94.3 1.4 collective-permute-start.10
  95.8 2.6 multiply_reduce_fusion.3
  99.4 105.0 %shard_map.152 = (f32[896,768]{1,0:T(8,128)S(1)}, f32[8,768]{1,0:T(8,128)S(1)}) custom-call(f32[896,768]{1,0:T(8,128)S(1)} %maximum_maximum_fusion.whole, f32[8,768]{1,0:T(8,128)S(1)} %concatenate.76.gains), custom_call_target="tpu_custom_call" | custom-call | bytes 200000000 | tf_op jit(solution)/shard_map/pallas_call | solution.py:235
  204.4 1.8 slice.164
  208.5 3.4 %collective-permute-done.12 = f32[512,768]{1,0:T(8,128)S(1)} collective-permute-done((f32[512,768]{1,0:T(8,128)S(1)}, f32[512,768]{1,0:T(8,128)S(1)}, u32[]{:S(2)}, u32[]{:S(2)}) %collective-permute-start.12) | collective-permute-done | bytes 1572896 | tf_op jit(solution)/shard_map/ppermute | solution.py:65
  212.2 1.1 copy-done.13
  214.0 1.9 multiply_reduce_fusion
  215.9 1.1 multiply_convert_fusion
  218.3 1.2 fusion.19
  219.5 1.5 fusion.6
  222.2 1.0 fusion.133
  223.2 1.0 fusion.134
  224.5 1.0 copy.36
  225.5 1.9 stack_reshape_reshape.4
  227.4 2.2 fusion.62
  229.8 1.0 copy-done.40
  230.8 0.8 convolution_bitcast_fusion.1
  231.8 3.3 %collective-permute-done.13 = f32[512,768]{1,0:T(8,128)S(1)} collective-permute-done((f32[512,768]{1,0:T(8,128)S(1)}, f32[512,768]{1,0:T(8,128)S(1)}, u32[]{:S(2)}, u32[]{:S(2)}) %collective-permute-start.13) | collective-permute-done | bytes 1572896 | tf_op jit(solution)/shard_map/ppermute | solution.py:65
  235.9 1.6 collective-permute-start.14
  239.1 1.3 multiply_reduce_fusion.2
  241.1 71.9 %shard_map.153 = (f32[768,768]{1,0:T(8,128)S(1)}, f32[8,768]{1,0:T(8,128)S(1)}) custom-call(f32[768,768]{1,0:T(8,128)S(1)} %pad_maximum_fusion.whole, f32[8,768]{1,0:T(8,128)S(1)} %concatenate.78.gains), custom_call_target="tpu_custom_call" | custom-call | bytes 200000000 | tf_op jit(solution)/shard_map/pallas_call | solution.py:235
  317.6 1.3 slice.173
  318.9 1.0 slice.174
  320.7 1.4 slice.171
  322.4 0.9 slice.172
  323.4 1.1 copy-done.34
  (217 shorter events, 29.4 us)
Async XLA Ops:
  0.6 71.9 %copy-start = (bf16[288,768]{1,0:T(8,128)(2,1)S(1)}, bf16[288,768]{1,0:T(8,128)(2,1)}, u32[]{:S(2)}) copy-start(bf16[288,768]{1,0:T(8,128)(2,1)} %param.14) | copy-start | bytes 1327108
  0.6 6.1 %copy-start.5 = (bf16[1024,768]{1,0:T(8,128)(2,1)S(1)}, bf16[1024,768]{1,0:T(8,128)(2,1)}, u32[]{:S(2)}) copy-start(bf16[1024,768]{1,0:T(8,128)(2,1)} %param.9) | copy-start | bytes 4718596
  4.9 2.4 copy-start.50
  4.9 2.4 copy-start.39
  11.2 1.1 copy-start.22
  14.5 2.3 copy-start.21
  16.8 1.1 copy-start.20
  16.9 1.2 copy-start.37
  18.8 1.8 copy-start.44
  18.8 1.8 copy-start.46
  20.4 1.3 copy-start.42
  20.6 1.2 copy-start.32
  21.8 2.1 copy-start.2
  23.9 2.4 copy-start.28
  26.8 4.2 %copy-start.38 = (bf16[192,768]{1,0:T(8,128)(2,1)S(1)}, bf16[192,768]{1,0:T(8,128)(2,1)}, u32[]{:S(2)}) copy-start(bf16[192,768]{1,0:T(8,128)(2,1)} %param.12) | copy-start | bytes 884740
  27.9 10.3 %collective-permute-start = (f32[512,192]{0,1:T(8,128)}, f32[512,192]{0,1:T(8,128)}, u32[]{:S(2)}, u32[]{:S(2)}) collective-permute-start(f32[512,192]{0,1:T(8,128)} %get-tuple-element.70), channel_id=1, source_target_pairs={{0,1},{1,0},{2,3},{3,2},{4,5},{5,4},{6,7},{7,6},{8,9},{9,8},{10,11... | collective-permute-start | bytes 1179656 | tf_op jit(solution)/shard_map/ppermute | solution.py:65
  28.4 34.8 %collective-permute-start.2 = (f32[512,192]{0,1:T(8,128)}, f32[512,192]{0,1:T(8,128)}, u32[]{:S(2)}, u32[]{:S(2)}) collective-permute-start(f32[512,192]{0,1:T(8,128)} %get-tuple-element.70), channel_id=1, source_target_pairs={{0,3},{1,2},{2,1},{3,0},{4,7},{5,6},{6,5},{7,4},{8,11},{9,10},{10,... | collective-permute-start | bytes 1179656 | tf_op jit(solution)/shard_map/ppermute | solution.py:65
  31.9 32.5 %collective-permute-start.3 = (f32[192,768]{1,0:T(8,128)}, f32[192,768]{1,0:T(8,128)}, u32[]{:S(2)}, u32[]{:S(2)}) collective-permute-start(f32[192,768]{1,0:T(8,128)} %convert_multiply_fusion), channel_id=1, source_target_pairs={{0,1},{1,0},{2,3},{3,2},{4,5},{5,4},{6,7},{7,6},{8,9},{9,8},{10,11... | collective-permute-start | bytes 1769480 | tf_op jit(solution)/shard_map/ppermute | solution.py:65
  31.9 31.2 %collective-permute-start.4 = (f32[192,768]{1,0:T(8,128)}, f32[192,768]{1,0:T(8,128)}, u32[]{:S(2)}, u32[]{:S(2)}) collective-permute-start(f32[192,768]{1,0:T(8,128)} %convert_multiply_fusion), channel_id=1, source_target_pairs={{0,2},{1,3},{2,0},{3,1},{4,6},{5,7},{6,4},{7,5},{8,10},{9,11},{10,... | collective-permute-start | bytes 1769480 | tf_op jit(solution)/shard_map/ppermute | solution.py:65
  32.3 29.8 %collective-permute-start.1 = (f32[512,192]{0,1:T(8,128)}, f32[512,192]{0,1:T(8,128)}, u32[]{:S(2)}, u32[]{:S(2)}) collective-permute-start(f32[512,192]{0,1:T(8,128)} %get-tuple-element.69), channel_id=1, source_target_pairs={{0,2},{1,3},{2,0},{3,1},{4,6},{5,7},{6,4},{7,5},{8,10},{9,11},{10,... | collective-permute-start | bytes 1179656 | tf_op jit(solution)/shard_map/ppermute | solution.py:65
  35.9 2.1 copy-start.49
  63.1 3.6 %copy-start.3 = (f32[1024,768]{1,0:T(8,128)S(1)}, f32[1024,768]{1,0:T(8,128)}, u32[]{:S(2)}) copy-start(f32[1024,768]{1,0:T(8,128)} %convert_element_type.132) | copy-start | bytes 9437188
  63.1 3.5 %collective-permute-start.5 = (f32[192,768]{1,0:T(8,128)}, f32[192,768]{1,0:T(8,128)S(1)}, u32[]{:S(2)}, u32[]{:S(2)}) collective-permute-start(f32[192,768]{1,0:T(8,128)} %collective-permute-done.4), channel_id=1, source_target_pairs={{0,1},{1,0},{2,3},{3,2},{4,5},{5,4},{6,7},{7,6},{8,9},{9,8},{10,11... | collective-permute-start | bytes 1769480 | tf_op jit(solution)/shard_map/ppermute | solution.py:65
  72.0 4.0 %collective-permute-start.6 = (f32[512,768]{1,0:T(8,128)}, f32[512,768]{1,0:T(8,128)}, u32[]{:S(2)}, u32[]{:S(2)}) collective-permute-start(f32[512,768]{1,0:T(8,128)} %get-tuple-element.51), channel_id=1, source_target_pairs={{0,1},{1,0},{2,3},{3,2},{4,5},{5,4},{6,7},{7,6},{8,9},{9,8},{10,11... | collective-permute-start | bytes 4718600 | tf_op jit(solution)/shard_map/ppermute | solution.py:65
  74.6 3.7 %copy-start.41 = (bf16[2,768,288]{1,2,0:T(8,128)(2,1)S(1)}, bf16[2,768,288]{1,2,0:T(8,128)(2,1)}, u32[]{:S(2)}) copy-start(bf16[2,768,288]{1,2,0:T(8,128)(2,1)} %param.13) | copy-start | bytes 2654212
  85.2 3.5 %collective-permute-start.7 = (f32[512,768]{1,0:T(8,128)S(1)}, f32[512,768]{1,0:T(8,128)S(1)}, u32[]{:S(2)}, u32[]{:S(2)}) collective-permute-start(f32[512,768]{1,0:T(8,128)S(1)} %convolution_bitcast_fusion.2), channel_id=1, source_target_pairs={{0,1},{1,0},{2,3},{3,2},{4,5},{5,4},{6,7},{7,6},{8,9},{9,8},{10,11... | collective-permute-start | bytes 4718600 | tf_op jit(solution)/shard_map/ppermute | solution.py:65
  90.1 3.5 %collective-permute-start.8 = (f32[512,768]{1,0:T(8,128)S(1)}, f32[512,768]{1,0:T(8,128)S(1)}, u32[]{:S(2)}, u32[]{:S(2)}) collective-permute-start(f32[512,768]{1,0:T(8,128)S(1)} %fusion.93), channel_id=1, source_target_pairs={{0,1},{1,0},{2,3},{3,2},{4,5},{5,4},{6,7},{7,6},{8,9},{9,8},{10,11... | collective-permute-start | bytes 4718600 | tf_op jit(solution)/shard_map/ppermute | solution.py:65
  90.6 115.6 %collective-permute-start.9 = (f32[512,768]{1,0:T(8,128)S(1)}, f32[512,768]{1,0:T(8,128)S(1)}, u32[]{:S(2)}, u32[]{:S(2)}) collective-permute-start(f32[512,768]{1,0:T(8,128)S(1)} %bitcast_add_fusion.1), channel_id=1, source_target_pairs={{0,2},{1,3},{2,0},{3,1},{4,6},{5,7},{6,4},{7,5},{8,10},{9,11},{10,... | collective-permute-start | bytes 4718600 | tf_op jit(solution)/shard_map/ppermute | solution.py:65
  94.3 4.2 %copy-start.11 = (f32[512,768]{1,0:T(8,128)}, f32[512,768]{1,0:T(8,128)S(1)}, u32[]{:S(2)}) copy-start(f32[512,768]{1,0:T(8,128)S(1)} %convolution_add_fusion) | copy-start | bytes 4718596
  94.3 111.9 %collective-permute-start.10 = (f32[512,768]{1,0:T(8,128)S(1)}, f32[512,768]{1,0:T(8,128)S(1)}, u32[]{:S(2)}, u32[]{:S(2)}) collective-permute-start(f32[512,768]{1,0:T(8,128)S(1)} %convolution_add_fusion), channel_id=1, source_target_pairs={{0,2},{1,3},{2,0},{3,1},{4,6},{5,7},{6,4},{7,5},{8,10},{9,11},{10,... | collective-permute-start | bytes 4718600 | tf_op jit(solution)/shard_map/ppermute | solution.py:65
  95.8 2.7 copy-start.7
  206.2 1.1 copy-start.30
  208.0 6.0 %slice-start = ((s8[4718592]{0:T(1024)(128)(4,1)}), s8[4194304]{0:T(1024)(128)(4,1)S(1)}, s32[]{:S(2)}) async-start(s8[4718592]{0:T(1024)(128)(4,1)} %bitcast.360), calls=%async_computation | async-start | bytes 8388608
  208.1 5.9 %slice-start.1 = ((s8[4718592]{0:T(1024)(128)(4,1)}), s8[524288]{0:T(1024)(128)(4,1)S(1)}, s32[]{:S(2)}) async-start(s8[4718592]{0:T(1024)(128)(4,1)} %bitcast.360), calls=%async_computation.1 | async-start | bytes 1048576
  208.4 3.7 %copy-start.15 = (f32[512,768]{1,0:T(8,128)}, f32[512,768]{1,0:T(8,128)S(1)}, u32[]{:S(2)}) copy-start(f32[512,768]{1,0:T(8,128)S(1)} %get-tuple-element.43) | copy-start | bytes 4718596
  208.4 3.5 %collective-permute-start.12 = (f32[512,768]{1,0:T(8,128)S(1)}, f32[512,768]{1,0:T(8,128)S(1)}, u32[]{:S(2)}, u32[]{:S(2)}) collective-permute-start(f32[512,768]{1,0:T(8,128)S(1)} %get-tuple-element.43), channel_id=1, source_target_pairs={{0,1},{1,0},{2,3},{3,2},{4,5},{5,4},{6,7},{7,6},{8,9},{9,8},{10,11... | collective-permute-start | bytes 4718600 | tf_op jit(solution)/shard_map/ppermute | solution.py:65
  212.2 1.2 copy-start.13
  212.2 1.8 copy-start.29
  215.9 1.1 copy-start.33
  217.0 1.0 copy-start.43
  217.0 1.1 copy-start.45
  217.0 1.2 copy-start.47
  219.4 1.7 copy-start.23
  221.1 1.1 copy-start.17
  224.3 3.1 copy-start.25
  227.4 2.2 copy-start.36
  229.6 1.2 copy-start.40
  230.8 6.8 %copy-start.12 = (f32[512,768]{1,0:T(8,128)S(1)}, f32[512,768]{1,0:T(8,128)}, u32[]{:S(2)}) copy-start(f32[512,768]{1,0:T(8,128)} %copy-done.11) | copy-start | bytes 4718596
  230.8 6.9 %copy-start.31 = (f32[512,768]{1,0:T(8,128)S(1)}, f32[512,768]{1,0:T(8,128)}, u32[]{:S(2)}) copy-start(f32[512,768]{1,0:T(8,128)} %copy-done.30) | copy-start | bytes 4718596
  231.6 3.5 %collective-permute-start.13 = (f32[512,768]{1,0:T(8,128)S(1)}, f32[512,768]{1,0:T(8,128)S(1)}, u32[]{:S(2)}, u32[]{:S(2)}) collective-permute-start(f32[512,768]{1,0:T(8,128)S(1)} %convolution_bitcast_fusion.1), channel_id=1, source_target_pairs={{0,1},{1,0},{2,3},{3,2},{4,5},{5,4},{6,7},{7,6},{8,9},{9,8},{10,11... | collective-permute-start | bytes 4718600 | tf_op jit(solution)/shard_map/ppermute | solution.py:65
  235.1 2.6 copy-start.4
  235.9 1.7 copy-start.10
  235.9 77.1 %collective-permute-start.14 = (f32[512,768]{1,0:T(8,128)S(1)}, f32[512,768]{1,0:T(8,128)S(1)}, u32[]{:S(2)}, u32[]{:S(2)}) collective-permute-start(f32[512,768]{1,0:T(8,128)S(1)} %bitcast_add_fusion), channel_id=1, source_target_pairs={{0,2},{1,3},{2,0},{3,1},{4,6},{5,7},{6,4},{7,5},{8,10},{9,11},{10,... | collective-permute-start | bytes 4718600 | tf_op jit(solution)/shard_map/ppermute | solution.py:65
  237.7 1.4 copy-start.6
  238.1 2.3 copy-start.14
  238.1 2.3 copy-start.19
  238.1 82.3 %collective-permute-start.11 = (f32[512,768]{1,0:T(8,128)S(1)}, f32[512,768]{1,0:T(8,128)S(1)}, u32[]{:S(2)}, u32[]{:S(2)}) collective-permute-start(f32[512,768]{1,0:T(8,128)S(1)} %get-tuple-element.47), channel_id=1, source_target_pairs={{0,1},{1,0},{2,3},{3,2},{4,5},{5,4},{6,7},{7,6},{8,9},{9,8},{10,11... | collective-permute-start | bytes 4718600 | tf_op jit(solution)/shard_map/ppermute | solution.py:65
  313.6 1.4 copy-start.16
  314.3 1.5 copy-start.8
  315.8 1.8 copy-start.9
  316.2 7.1 %collective-permute-start.15 = (f32[512,768]{1,0:T(8,128)S(1)}, f32[512,768]{1,0:T(8,128)S(1)}, u32[]{:S(2)}, u32[]{:S(2)}) collective-permute-start(f32[512,768]{1,0:T(8,128)S(1)} %get-tuple-element.39), channel_id=1, source_target_pairs={{0,1},{1,0},{2,3},{3,2},{4,5},{5,4},{6,7},{7,6},{8,9},{9,8},{10,11... | collective-permute-start | bytes 4718600 | tf_op jit(solution)/shard_map/ppermute | solution.py:65
  320.7 1.7 copy-start.35
  323.2 1.3 copy-start.1
  323.4 1.1 copy-start.34
  (5 other events, 3.9 us)

commit v5 on v4

--- a/solution.py
+++ b/solution.py
@@ -91,13 +91,13 @@
 def chains_of(rows, dp_size):
     unit = 8 * dp_size
     units = rows // unit
-    count = min(4, units)
+    count = min(6, units)
     masks = masks_of(dp_size)
     chains = []
     start = 0
     for index in range(count):
         size = (units // count + (1 if index >= count - units % count else 0)) * unit
-        order = masks[1:] + masks[:1] if index == 1 else masks
+        order = masks[1:2] + masks[:1] + masks[2:] if index % 2 else masks
         chains.append((start, size, order))
         start += size
     return chains

time: 325 us -> 314 us (0.966)
  Pallas kernels: 177 us -> 166 us
    pallas_call x2, Pallas kernels: 177 us -> 166 us  [dp_sum(): pl.pallas_call(functools.partial(sum_kernel, dp_size), out_shape=(jax.Sha...]
  transfers between devices with their start and end apart: 16 -> 16, of which waited for: 6 -> 6; matrix products, arithmetic and copies ran while one was open for 9% -> 9% of each run, Pallas kernels for 55% -> 53%
where the time goes in v5:
time: 314 us; the launch traced here: 313 us
  Pallas kernels  166 us (53%)
  other arithmetic  36.9 us (12%)
  waiting for transfers between devices  35.5 us (11%)
  local copies, waits for them, and re-layouts  34.1 us (11%)
  matrix products  26.8 us (9%)
  starting transfers between devices  11.5 us (4%)
    pallas_call x2, Pallas kernels, dp_sum(): pl.pallas_call(functools.partial(sum_kernel, dp_size), out_shape=(jax.Sha...  166 us
    ppermute x16, waiting for transfers between devices, swap(): return lax.ppermute(array, axis, [(i, i ^ mask) for i in range(size)])  35.5 us
    unnamed x119, local copies, waits for them, and re-layouts  15.7 us
    ppermute x16, starting transfers between devices, swap(): return lax.ppermute(array, axis, [(i, i ^ mask) for i in range(size)])  11.5 us
  transfers between devices with their start and end apart: 16, of which 6 were waited for; matrix products, arithmetic and copies ran while one was open for 9% of the time, Pallas kernels for 53%

profile of v5, /device:TPU:0, one launch (start us, length us, event | category | flops | bytes accessed | tf_op | source)
XLA Modules:
  0.0 313.2 jit_solution(172277798513533093)
XLA Ops:
  0.7 1.3 slice.149
  2.7 0.9 select_bitcast_fusion
  5.0 1.8 convert_reduce_fusion
  7.4 1.3 fusion.126
  8.7 1.6 slice_bitcast_fusion.3
  11.4 0.9 copy-done.22
  12.5 1.1 fusion.99
  14.6 1.9 fusion.97
  17.1 0.9 copy-done.20
  19.2 1.0 fusion.18
  20.6 1.1 fusion.135
  21.8 1.2 fusion
  23.9 2.4 multiply_bitcast_fusion.1
  27.0 0.9 constant_dynamic-slice_fusion
  28.4 2.6 collective-permute-start.2
  31.0 0.9 convert_multiply_fusion
  32.3 1.6 collective-permute-start.1
  34.0 1.9 convert_element_type.132
  35.9 1.3 copy.31
  38.2 1.0 fusion.103
  39.2 22.8 %collective-permute-done.1 = f32[512,192]{0,1:T(8,128)} collective-permute-done((f32[512,192]{0,1:T(8,128)}, f32[512,192]{0,1:T(8,128)}, u32[]{:S(2)}, u32[]{:S(2)}) %collective-permute-start.1) | collective-permute-done | bytes 393248 | tf_op jit(solution)/shard_map/ppermute | solution.py:65
  62.1 1.0 fusion.105
  63.2 1.2 fusion.107
  64.4 1.1 fusion.88
  65.5 1.1 fusion.90
  66.7 2.0 fusion.130
  69.0 1.3 broadcast.282.clone.1
  70.3 1.7 fusion.42
  72.6 2.1 fusion.136
  74.7 1.3 collective-permute-done.6
  76.0 2.4 fusion.44
  78.4 2.5 convolution_bitcast_fusion
  80.9 2.8 multiply_convert_fusion.4
  84.4 0.8 convolution_bitcast_fusion.2
  85.6 3.0 collective-permute-done.7
  88.7 0.8 bitcast_add_fusion.1
  90.6 1.4 collective-permute-start.9
  91.9 1.7 collective-permute-done.8
  94.3 1.4 collective-permute-start.10
  95.8 2.6 multiply_reduce_fusion.3
  99.4 101.0 %shard_map.152 = (f32[896,768]{1,0:T(8,128)S(1)}, f32[8,768]{1,0:T(8,128)S(1)}) custom-call(f32[896,768]{1,0:T(8,128)S(1)} %maximum_maximum_fusion.whole, f32[8,768]{1,0:T(8,128)S(1)} %concatenate.76.gains), custom_call_target="tpu_custom_call" | custom-call | bytes 200000000 | tf_op jit(solution)/shard_map/pallas_call | solution.py:235
  200.4 1.8 slice.164
  204.5 3.4 %collective-permute-done.12 = f32[512,768]{1,0:T(8,128)S(1)} collective-permute-done((f32[512,768]{1,0:T(8,128)S(1)}, f32[512,768]{1,0:T(8,128)S(1)}, u32[]{:S(2)}, u32[]{:S(2)}) %collective-permute-start.12) | collective-permute-done | bytes 1572896 | tf_op jit(solution)/shard_map/ppermute | solution.py:65
  208.1 1.1 copy-done.13
  210.0 1.9 multiply_reduce_fusion
  211.8 1.1 multiply_convert_fusion
  214.2 1.2 fusion.19
  215.4 1.5 fusion.6
  218.2 1.0 fusion.133
  219.1 1.0 fusion.134
  220.4 1.0 copy.36
  221.5 1.9 stack_reshape_reshape.4
  223.4 2.2 fusion.62
  225.7 1.0 copy-done.40
  226.7 0.8 convolution_bitcast_fusion.1
  227.8 3.3 %collective-permute-done.13 = f32[512,768]{1,0:T(8,128)S(1)} collective-permute-done((f32[512,768]{1,0:T(8,128)S(1)}, f32[512,768]{1,0:T(8,128)S(1)}, u32[]{:S(2)}, u32[]{:S(2)}) %collective-permute-start.13) | collective-permute-done | bytes 1572896 | tf_op jit(solution)/shard_map/ppermute | solution.py:65
  231.9 1.5 collective-permute-start.14
  235.0 1.3 multiply_reduce_fusion.2
  237.0 64.6 %shard_map.153 = (f32[768,768]{1,0:T(8,128)S(1)}, f32[8,768]{1,0:T(8,128)S(1)}) custom-call(f32[768,768]{1,0:T(8,128)S(1)} %pad_maximum_fusion.whole, f32[8,768]{1,0:T(8,128)S(1)} %concatenate.78.gains), custom_call_target="tpu_custom_call" | custom-call | bytes 200000000 | tf_op jit(solution)/shard_map/pallas_call | solution.py:235
  306.2 1.3 slice.173
  307.5 1.0 slice.174
  309.3 1.4 slice.171
  311.0 0.9 slice.172
  312.0 1.1 copy-done.34
  (217 shorter events, 29.5 us)
Async XLA Ops:
  0.6 71.9 %copy-start = (bf16[288,768]{1,0:T(8,128)(2,1)S(1)}, bf16[288,768]{1,0:T(8,128)(2,1)}, u32[]{:S(2)}) copy-start(bf16[288,768]{1,0:T(8,128)(2,1)} %param.14) | copy-start | bytes 1327108
  0.6 6.1 %copy-start.5 = (bf16[1024,768]{1,0:T(8,128)(2,1)S(1)}, bf16[1024,768]{1,0:T(8,128)(2,1)}, u32[]{:S(2)}) copy-start(bf16[1024,768]{1,0:T(8,128)(2,1)} %param.9) | copy-start | bytes 4718596
  4.9 2.4 copy-start.50
  4.9 2.4 copy-start.39
  11.2 1.1 copy-start.22
  14.5 2.3 copy-start.21
  16.8 1.1 copy-start.20
  16.9 1.2 copy-start.37
  18.8 1.8 copy-start.44
  18.8 1.8 copy-start.46
  20.4 1.3 copy-start.42
  20.6 1.2 copy-start.32
  21.8 2.1 copy-start.2
  23.9 2.4 copy-start.28
  26.8 4.2 %copy-start.38 = (bf16[192,768]{1,0:T(8,128)(2,1)S(1)}, bf16[192,768]{1,0:T(8,128)(2,1)}, u32[]{:S(2)}) copy-start(bf16[192,768]{1,0:T(8,128)(2,1)} %param.12) | copy-start | bytes 884740
  27.9 10.3 %collective-permute-start = (f32[512,192]{0,1:T(8,128)}, f32[512,192]{0,1:T(8,128)}, u32[]{:S(2)}, u32[]{:S(2)}) collective-permute-start(f32[512,192]{0,1:T(8,128)} %get-tuple-element.70), channel_id=1, source_target_pairs={{0,1},{1,0},{2,3},{3,2},{4,5},{5,4},{6,7},{7,6},{8,9},{9,8},{10,11... | collective-permute-start | bytes 1179656 | tf_op jit(solution)/shard_map/ppermute | solution.py:65
  28.4 34.8 %collective-permute-start.2 = (f32[512,192]{0,1:T(8,128)}, f32[512,192]{0,1:T(8,128)}, u32[]{:S(2)}, u32[]{:S(2)}) collective-permute-start(f32[512,192]{0,1:T(8,128)} %get-tuple-element.70), channel_id=1, source_target_pairs={{0,3},{1,2},{2,1},{3,0},{4,7},{5,6},{6,5},{7,4},{8,11},{9,10},{10,... | collective-permute-start | bytes 1179656 | tf_op jit(solution)/shard_map/ppermute | solution.py:65
  31.9 32.5 %collective-permute-start.3 = (f32[192,768]{1,0:T(8,128)}, f32[192,768]{1,0:T(8,128)}, u32[]{:S(2)}, u32[]{:S(2)}) collective-permute-start(f32[192,768]{1,0:T(8,128)} %convert_multiply_fusion), channel_id=1, source_target_pairs={{0,1},{1,0},{2,3},{3,2},{4,5},{5,4},{6,7},{7,6},{8,9},{9,8},{10,11... | collective-permute-start | bytes 1769480 | tf_op jit(solution)/shard_map/ppermute | solution.py:65
  31.9 31.2 %collective-permute-start.4 = (f32[192,768]{1,0:T(8,128)}, f32[192,768]{1,0:T(8,128)}, u32[]{:S(2)}, u32[]{:S(2)}) collective-permute-start(f32[192,768]{1,0:T(8,128)} %convert_multiply_fusion), channel_id=1, source_target_pairs={{0,2},{1,3},{2,0},{3,1},{4,6},{5,7},{6,4},{7,5},{8,10},{9,11},{10,... | collective-permute-start | bytes 1769480 | tf_op jit(solution)/shard_map/ppermute | solution.py:65
  32.3 29.8 %collective-permute-start.1 = (f32[512,192]{0,1:T(8,128)}, f32[512,192]{0,1:T(8,128)}, u32[]{:S(2)}, u32[]{:S(2)}) collective-permute-start(f32[512,192]{0,1:T(8,128)} %get-tuple-element.69), channel_id=1, source_target_pairs={{0,2},{1,3},{2,0},{3,1},{4,6},{5,7},{6,4},{7,5},{8,10},{9,11},{10,... | collective-permute-start | bytes 1179656 | tf_op jit(solution)/shard_map/ppermute | solution.py:65
  35.9 2.1 copy-start.49
  63.1 3.6 %copy-start.3 = (f32[1024,768]{1,0:T(8,128)S(1)}, f32[1024,768]{1,0:T(8,128)}, u32[]{:S(2)}) copy-start(f32[1024,768]{1,0:T(8,128)} %convert_element_type.132) | copy-start | bytes 9437188
  63.1 3.5 %collective-permute-start.5 = (f32[192,768]{1,0:T(8,128)}, f32[192,768]{1,0:T(8,128)S(1)}, u32[]{:S(2)}, u32[]{:S(2)}) collective-permute-start(f32[192,768]{1,0:T(8,128)} %collective-permute-done.4), channel_id=1, source_target_pairs={{0,1},{1,0},{2,3},{3,2},{4,5},{5,4},{6,7},{7,6},{8,9},{9,8},{10,11... | collective-permute-start | bytes 1769480 | tf_op jit(solution)/shard_map/ppermute | solution.py:65
  72.0 4.0 %collective-permute-start.6 = (f32[512,768]{1,0:T(8,128)}, f32[512,768]{1,0:T(8,128)}, u32[]{:S(2)}, u32[]{:S(2)}) collective-permute-start(f32[512,768]{1,0:T(8,128)} %get-tuple-element.51), channel_id=1, source_target_pairs={{0,1},{1,0},{2,3},{3,2},{4,5},{5,4},{6,7},{7,6},{8,9},{9,8},{10,11... | collective-permute-start | bytes 4718600 | tf_op jit(solution)/shard_map/ppermute | solution.py:65
  74.6 3.7 %copy-start.41 = (bf16[2,768,288]{1,2,0:T(8,128)(2,1)S(1)}, bf16[2,768,288]{1,2,0:T(8,128)(2,1)}, u32[]{:S(2)}) copy-start(bf16[2,768,288]{1,2,0:T(8,128)(2,1)} %param.13) | copy-start | bytes 2654212
  85.2 3.5 %collective-permute-start.7 = (f32[512,768]{1,0:T(8,128)S(1)}, f32[512,768]{1,0:T(8,128)S(1)}, u32[]{:S(2)}, u32[]{:S(2)}) collective-permute-start(f32[512,768]{1,0:T(8,128)S(1)} %convolution_bitcast_fusion.2), channel_id=1, source_target_pairs={{0,1},{1,0},{2,3},{3,2},{4,5},{5,4},{6,7},{7,6},{8,9},{9,8},{10,11... | collective-permute-start | bytes 4718600 | tf_op jit(solution)/shard_map/ppermute | solution.py:65
  90.1 3.5 %collective-permute-start.8 = (f32[512,768]{1,0:T(8,128)S(1)}, f32[512,768]{1,0:T(8,128)S(1)}, u32[]{:S(2)}, u32[]{:S(2)}) collective-permute-start(f32[512,768]{1,0:T(8,128)S(1)} %fusion.93), channel_id=1, source_target_pairs={{0,1},{1,0},{2,3},{3,2},{4,5},{5,4},{6,7},{7,6},{8,9},{9,8},{10,11... | collective-permute-start | bytes 4718600 | tf_op jit(solution)/shard_map/ppermute | solution.py:65
  90.6 111.5 %collective-permute-start.9 = (f32[512,768]{1,0:T(8,128)S(1)}, f32[512,768]{1,0:T(8,128)S(1)}, u32[]{:S(2)}, u32[]{:S(2)}) collective-permute-start(f32[512,768]{1,0:T(8,128)S(1)} %bitcast_add_fusion.1), channel_id=1, source_target_pairs={{0,2},{1,3},{2,0},{3,1},{4,6},{5,7},{6,4},{7,5},{8,10},{9,11},{10,... | collective-permute-start | bytes 4718600 | tf_op jit(solution)/shard_map/ppermute | solution.py:65
  94.3 4.2 %copy-start.11 = (f32[512,768]{1,0:T(8,128)}, f32[512,768]{1,0:T(8,128)S(1)}, u32[]{:S(2)}) copy-start(f32[512,768]{1,0:T(8,128)S(1)} %convolution_add_fusion) | copy-start | bytes 4718596
  94.3 107.9 %collective-permute-start.10 = (f32[512,768]{1,0:T(8,128)S(1)}, f32[512,768]{1,0:T(8,128)S(1)}, u32[]{:S(2)}, u32[]{:S(2)}) collective-permute-start(f32[512,768]{1,0:T(8,128)S(1)} %convolution_add_fusion), channel_id=1, source_target_pairs={{0,2},{1,3},{2,0},{3,1},{4,6},{5,7},{6,4},{7,5},{8,10},{9,11},{10,... | collective-permute-start | bytes 4718600 | tf_op jit(solution)/shard_map/ppermute | solution.py:65
  95.8 2.7 copy-start.7
  202.1 1.1 copy-start.30
  204.0 6.0 %slice-start = ((s8[4718592]{0:T(1024)(128)(4,1)}), s8[4194304]{0:T(1024)(128)(4,1)S(1)}, s32[]{:S(2)}) async-start(s8[4718592]{0:T(1024)(128)(4,1)} %bitcast.360), calls=%async_computation | async-start | bytes 8388608
  204.1 5.9 %slice-start.1 = ((s8[4718592]{0:T(1024)(128)(4,1)}), s8[524288]{0:T(1024)(128)(4,1)S(1)}, s32[]{:S(2)}) async-start(s8[4718592]{0:T(1024)(128)(4,1)} %bitcast.360), calls=%async_computation.1 | async-start | bytes 1048576
  204.4 3.7 %copy-start.15 = (f32[512,768]{1,0:T(8,128)}, f32[512,768]{1,0:T(8,128)S(1)}, u32[]{:S(2)}) copy-start(f32[512,768]{1,0:T(8,128)S(1)} %get-tuple-element.43) | copy-start | bytes 4718596
  204.4 3.5 %collective-permute-start.12 = (f32[512,768]{1,0:T(8,128)S(1)}, f32[512,768]{1,0:T(8,128)S(1)}, u32[]{:S(2)}, u32[]{:S(2)}) collective-permute-start(f32[512,768]{1,0:T(8,128)S(1)} %get-tuple-element.43), channel_id=1, source_target_pairs={{0,1},{1,0},{2,3},{3,2},{4,5},{5,4},{6,7},{7,6},{8,9},{9,8},{10,11... | collective-permute-start | bytes 4718600 | tf_op jit(solution)/shard_map/ppermute | solution.py:65
  208.1 1.2 copy-start.13
  208.1 1.8 copy-start.29
  211.8 1.1 copy-start.33
  213.0 1.0 copy-start.43
  213.0 1.1 copy-start.45
  213.0 1.2 copy-start.47
  215.4 1.7 copy-start.23
  217.1 1.1 copy-start.17
  220.3 3.1 copy-start.25
  223.4 2.2 copy-start.36
  225.6 1.2 copy-start.40
  226.7 6.8 %copy-start.12 = (f32[512,768]{1,0:T(8,128)S(1)}, f32[512,768]{1,0:T(8,128)}, u32[]{:S(2)}) copy-start(f32[512,768]{1,0:T(8,128)} %copy-done.11) | copy-start | bytes 4718596
  226.7 6.8 %copy-start.31 = (f32[512,768]{1,0:T(8,128)S(1)}, f32[512,768]{1,0:T(8,128)}, u32[]{:S(2)}) copy-start(f32[512,768]{1,0:T(8,128)} %copy-done.30) | copy-start | bytes 4718596
  227.6 3.5 %collective-permute-start.13 = (f32[512,768]{1,0:T(8,128)S(1)}, f32[512,768]{1,0:T(8,128)S(1)}, u32[]{:S(2)}, u32[]{:S(2)}) collective-permute-start(f32[512,768]{1,0:T(8,128)S(1)} %convolution_bitcast_fusion.1), channel_id=1, source_target_pairs={{0,1},{1,0},{2,3},{3,2},{4,5},{5,4},{6,7},{7,6},{8,9},{9,8},{10,11... | collective-permute-start | bytes 4718600 | tf_op jit(solution)/shard_map/ppermute | solution.py:65
  231.1 2.5 copy-start.4
  231.9 1.7 copy-start.10
  231.9 69.8 %collective-permute-start.14 = (f32[512,768]{1,0:T(8,128)S(1)}, f32[512,768]{1,0:T(8,128)S(1)}, u32[]{:S(2)}, u32[]{:S(2)}) collective-permute-start(f32[512,768]{1,0:T(8,128)S(1)} %bitcast_add_fusion), channel_id=1, source_target_pairs={{0,2},{1,3},{2,0},{3,1},{4,6},{5,7},{6,4},{7,5},{8,10},{9,11},{10,... | collective-permute-start | bytes 4718600 | tf_op jit(solution)/shard_map/ppermute | solution.py:65
  233.6 1.4 copy-start.6
  234.0 2.3 copy-start.14
  234.1 2.3 copy-start.19
  234.1 75.0 %collective-permute-start.11 = (f32[512,768]{1,0:T(8,128)S(1)}, f32[512,768]{1,0:T(8,128)S(1)}, u32[]{:S(2)}, u32[]{:S(2)}) collective-permute-start(f32[512,768]{1,0:T(8,128)S(1)} %get-tuple-element.47), channel_id=1, source_target_pairs={{0,1},{1,0},{2,3},{3,2},{4,5},{5,4},{6,7},{7,6},{8,9},{9,8},{10,11... | collective-permute-start | bytes 4718600 | tf_op jit(solution)/shard_map/ppermute | solution.py:65
  302.2 1.4 copy-start.16
  302.9 1.5 copy-start.8
  304.4 1.8 copy-start.9
  304.8 7.1 %collective-permute-start.15 = (f32[512,768]{1,0:T(8,128)S(1)}, f32[512,768]{1,0:T(8,128)S(1)}, u32[]{:S(2)}, u32[]{:S(2)}) collective-permute-start(f32[512,768]{1,0:T(8,128)S(1)} %get-tuple-element.39), channel_id=1, source_target_pairs={{0,1},{1,0},{2,3},{3,2},{4,5},{5,4},{6,7},{7,6},{8,9},{9,8},{10,11... | collective-permute-start | bytes 4718600 | tf_op jit(solution)/shard_map/ppermute | solution.py:65
  309.3 1.7 copy-start.35
  311.8 1.3 copy-start.1
  312.0 1.1 copy-start.34
  (5 other events, 3.9 us)
